TPU v7x, 128 devices: a whole 4x4x4 slice. The times are simulated.
128 devices in a mesh: ctx: 8 (over y, core), exp: 16 (over z, x).
Axes of the slice: x: 4, y: 4, z: 4, core: 2. Of those that a mesh axis runs over, the one named last changes fastest.
Arguments:
- stream_in: bfloat16 [16, 1024, 2560], P('exp', 'ctx'), may hold values from -1.75 to 1.75
- queries: bfloat16 [16, 1024, 12288], P('exp', 'ctx'), may hold values from -8 to 8
- latents: bfloat16 [16, 1024, 512], P('exp', 'ctx'), may hold values from -6 to 6
- key_rope: bfloat16 [16, 1024, 64], P('exp', 'ctx'), may hold values from -8 to 8
- w_uk: bfloat16 [512, 8192], P(None, 'ctx'), may hold values from -0.25 to 0.25
- w_uv: bfloat16 [512, 8192], P(None, 'ctx'), may hold values from -0.25 to 0.25
- w_o: bfloat16 [8192, 2560], P('ctx'), may hold values from -0.1875 to 0.1875
- norm_gain: float32 [2560], replicated, may hold values from 0.25 to 1.75
- expert_ids: int32 [16, 1024, 6], P('exp', 'ctx'), may hold values from 0 to 127, all different within a row; in each aligned block of 128 rows (0 to 127, 128 to 255, ..., all dimensions but the last counted through in order) at most 9 rows name the same one
- gate_weights: float32 [16, 1024, 6], P('exp', 'ctx'), may hold values from 0.05 to 0.45
- w_gate: bfloat16 [128, 2560, 768], P(('ctx', 'exp')), may hold values from -0.125 to 0.125
- w_up: bfloat16 [128, 2560, 768], P(('ctx', 'exp')), may hold values from -0.125 to 0.125
- w_down: bfloat16 [128, 768, 2560], P(('ctx', 'exp')), may hold values from -0.21875 to 0.21875
Outputs:
- layer_out: bfloat16 [16, 1024, 2560], P('exp', 'ctx')
Inputs may be any that keep to these rules, and one draw needn't show every extreme that they name: `expert_ids`: each position names 6 different experts; among the positions of one source no expert is named more than 9 times, and in some sources an expert is named exactly 9 times.
All inputs are finite; a program needn't handle non-finite values.
Results may differ from a plain program's by a relative error of at most 0.023.
Values may be sent and summed in bfloat16 or wider, within the bound.
A program may use at most 128 MiB of HBM per device.

v0:
```python
import math

import jax
import jax.numpy as jnp
from jax import lax
from jax.sharding import PartitionSpec as P

NOPE = 128
ROPE = 64
VDIM = 128
TOPK = 6


def local(
    stream_in,
    queries,
    latents,
    key_rope,
    w_uk,
    w_uv,
    w_o,
    norm_gain,
    expert_ids,
    gate_weights,
    w_gate,
    w_up,
    w_down,
):
    ctx_size = lax.axis_size("ctx")
    exp_size = lax.axis_size("exp")
    tok_rows = stream_in.shape[1]
    model_width = stream_in.shape[2]
    length = tok_rows * ctx_size
    heads_here = w_uk.shape[1] // NOPE
    local_queries = lax.all_to_all(queries[0], "ctx", split_axis=1, concat_axis=0, tiled=True)
    all_latent, all_rope = (
        lax.all_gather(latents[0], "ctx", axis=0, tiled=True),
        lax.all_gather(key_rope[0], "ctx", axis=0, tiled=True),
    )
    keys_nope = jnp.dot(all_latent, w_uk, preferred_element_type=jnp.float32).astype(jnp.bfloat16)
    values = jnp.dot(all_latent, w_uv, preferred_element_type=jnp.float32).astype(jnp.bfloat16)
    head_queries = local_queries.reshape(length, heads_here, NOPE + ROPE).transpose(1, 0, 2)
    head_keys = keys_nope.reshape(length, heads_here, NOPE).transpose(1, 0, 2)
    head_values = values.reshape(length, heads_here, VDIM).transpose(1, 0, 2)
    score_scale = 1.0 / math.sqrt(NOPE + ROPE)
    block_rows = min(512, length)
    pieces = []
    for block_start in range(0, length, block_rows):
        key_end = block_start + block_rows
        causal = (block_start + jnp.arange(block_rows))[:, None] >= jnp.arange(key_end)[None, :]
        rope_keys = all_rope[:key_end]

        def one_head(head_parts):
            one_query, key_nope, one_value = head_parts
            key_full = jnp.concatenate([key_nope, rope_keys], axis=1)
            scores = (
                jnp.dot(one_query, key_full.T, preferred_element_type=jnp.float32) * score_scale
            )
            scores = jnp.where(causal, scores, -jnp.inf)
            row_peak = jnp.max(scores, axis=1, keepdims=True)
            weights = jnp.exp(scores - row_peak)
            weights = (weights / jnp.sum(weights, axis=1, keepdims=True)).astype(jnp.bfloat16)
            return jnp.dot(weights, one_value, preferred_element_type=jnp.float32).astype(
                jnp.bfloat16
            )

        pieces.append(
            lax.map(
                one_head,
                (
                    head_queries[:, block_start:key_end],
                    head_keys[:, :key_end],
                    head_values[:, :key_end],
                ),
            )
        )
    heads_out = jnp.concatenate(pieces, axis=1)
    mixed_heads = heads_out.transpose(1, 0, 2).reshape(length, heads_here * VDIM)
    attention = lax.psum_scatter(
        jnp.dot(mixed_heads, w_o, preferred_element_type=jnp.float32).astype(jnp.bfloat16),
        "ctx",
        scatter_dimension=0,
        tiled=True,
    ).astype(jnp.float32)
    hidden = (stream_in[0].astype(jnp.float32) + attention).astype(jnp.bfloat16)
    hidden_f = hidden.astype(jnp.float32)
    mean_square = jnp.mean(hidden_f * hidden_f, axis=-1, keepdims=True)
    normed = (hidden_f * lax.rsqrt(mean_square + 1e-06) * norm_gain).astype(jnp.bfloat16)
    experts_all = ctx_size * exp_size
    capacity = max(2, 3 * tok_rows * TOPK // (2 * experts_all))
    pairs = tok_rows * TOPK
    route_ids = expert_ids[0].reshape(pairs)
    onehot = (route_ids[:, None] == jnp.arange(experts_all)[None, :]).astype(jnp.float32)
    lower_tri = (jnp.arange(pairs)[:, None] >= jnp.arange(pairs)[None, :]).astype(jnp.float32)
    counts = jnp.dot(lower_tri, onehot, precision=lax.Precision.HIGHEST)
    slot_index = (jnp.sum(onehot * counts, axis=1) - 1.0).astype(jnp.int32)
    target_row = route_ids * capacity + slot_index
    token_index = jnp.arange(pairs, dtype=jnp.int32) // TOPK
    source_row = jnp.zeros((experts_all * capacity,), jnp.int32).at[target_row].set(token_index)
    filled = jnp.zeros((experts_all * capacity,), jnp.bfloat16).at[target_row].set(1.0)
    outgoing = (normed[source_row] * filled[:, None]).reshape(experts_all, capacity, model_width)
    arrived = lax.all_to_all(outgoing, ("ctx", "exp"), split_axis=0, concat_axis=0, tiled=True)
    flat_rows = arrived.reshape(-1, model_width)
    gate_part = jnp.dot(flat_rows, w_gate[0], preferred_element_type=jnp.float32)
    up_part = jnp.dot(flat_rows, w_up[0], preferred_element_type=jnp.float32)
    active = (jax.nn.silu(gate_part) * up_part).astype(jnp.bfloat16)
    result = jnp.dot(active, w_down[0], preferred_element_type=jnp.float32).astype(jnp.bfloat16)
    returned = lax.all_to_all(
        result.reshape(arrived.shape), ("ctx", "exp"), split_axis=0, concat_axis=0, tiled=True
    )
    picked = returned.reshape(experts_all * capacity, model_width)[target_row].reshape(
        tok_rows, TOPK, model_width
    )
    combined = jnp.sum(gate_weights[0][:, :, None] * picked.astype(jnp.float32), axis=1)
    layer_out = (hidden.astype(jnp.float32) + combined).astype(jnp.bfloat16)
    return layer_out[None]


def solution(mesh):
    return jax.shard_map(
        local,
        mesh=mesh,
        in_specs=(
            P("exp", "ctx", None),
            P("exp", "ctx", None),
            P("exp", "ctx", None),
            P("exp", "ctx", None),
            P(None, "ctx"),
            P(None, "ctx"),
            P("ctx", None),
            P(),
            P("exp", "ctx", None),
            P("exp", "ctx", None),
            P(("ctx", "exp"), None, None),
            P(("ctx", "exp"), None, None),
            P(("ctx", "exp"), None, None),
        ),
        out_specs=P("exp", "ctx", None),
        check_vma=False,
    )
```

profile of v0, /device:TPU:34, one launch (start us, length us, event | category | flops | bytes accessed | tf_op | source)
XLA Modules:
  0.0 622.8 jit_solution(6741106481387860059)
XLA Ops:
  6.5 4.8 copy.29
  11.3 4.6 all-to-all-start
  16.8 47.8 %all-gather.1 = bf16[1,1024,64]{2,1,0:T(8,128)(2,1)S(1)} all-gather(bf16[1,128,64]{2,1,0:T(8,128)(2,1)S(1)} %copy.32), channel_id=3, replica_groups=mesh['ctx'=8,'exp'=16] {'ctx'}, dimensions={1}, use_global_device_ids=true | all-gather | bytes 147456 | tf_op jit(solution)/shard_map/all_gather | solution.py:38
  65.3 3.9 convolution_convert_fusion.5
  69.2 3.1 copy.31
  73.4 3.9 convolution_convert_fusion.4
  77.3 3.9 copy.33
  81.2 2.4 slice.28
  83.6 10.7 %copy.30 = bf16[8,128,1536]{1,0,2:T(8,128)(2,1)} copy(bf16[8,128,1536]{1,2,0:T(8,128)(2,1)} %bitcast.2) | data formatting | bytes 6291456 | tf_op jit(solution)/shard_map/all_to_all | solution.py:35
  94.3 5.8 reshape.95
  100.1 3.9 fusion.61
  105.0 35.9 %while.22 = (s32[]{:T(128)}, bf16[8,512,128]{1,2,0:T(8,128)(2,1)}, bf16[8,512,192]{1,2,0:T(8,128)(2,1)}, bf16[8,512,128]{2,1,0:T(8,128)(2,1)}, bf16[512,64]{1,0:...) while((s32[]{:T(128)}, bf16[8,512,128]{1,2,0:T(8,128)(2,1)}, ...), condition=%wide.region_3.4_spmd.clone, body=%wide.region_0.3_spmd.clone.sunk | while | flops 170589184 | bytes 4664913 | solution.py:68
  105.9 1.3 fusion.77
  107.5 1.3 fusion.79
  110.4 1.3 fusion.77
  111.9 1.3 fusion.79
  114.9 1.3 fusion.77
  116.4 1.3 fusion.79
  119.4 1.3 fusion.77
  120.9 1.3 fusion.79
  123.9 1.3 fusion.77
  125.4 1.3 fusion.79
  128.4 1.3 fusion.77
  129.9 1.3 fusion.79
  132.9 1.3 fusion.77
  137.4 1.3 fusion.77
  142.1 36.2 %while.23 = (s32[]{:T(128)}, bf16[8,512,128]{1,2,0:T(8,128)(2,1)}, bf16[8,512,192]{1,2,0:T(8,128)(2,1)}, bf16[8,1024,128]{2,1,0:T(8,128)(2,1)S(1)}, bf16[1024,64...) while((s32[]{:T(128)}, bf16[8,512,128]{1,2,0:T(8,128)(2,1)}, ...), condition=%wide.region_7.8_spmd.clone, body=%wide.region_4.7_spmd.clone.sunk | while | flops 341113856 | bytes 8336985 | solution.py:68
  142.1 1.7 fusion.81
  144.3 1.5 fusion.83
  146.6 1.7 fusion.81
  148.8 1.5 fusion.83
  151.1 1.7 fusion.81
  153.4 1.5 fusion.83
  155.7 1.7 fusion.81
  157.9 1.5 fusion.83
  160.2 1.7 fusion.81
  162.4 1.5 fusion.83
  164.7 1.7 fusion.81
  166.9 1.5 fusion.83
  169.3 1.7 fusion.81
  171.5 1.5 fusion.83
  173.8 1.7 fusion.81
  176.0 1.5 fusion.83
  178.3 1.8 pad_maximum_fusion
  180.1 10.1 %convolution_convert_fusion.3 = bf16[1024,2560]{1,0:T(8,128)(2,1)} fusion(bf16[1024,1024]{0,1:T(8,128)(2,1)S(1)} %bitcast.99, bf16[1024,2560]{1,0:T(8,128)(2,1)} %param.23), kind=kOutput, calls=%fused_computation.47 | convolution fusion | flops 5371330560 | bytes 12582912 | tf_op jit(solution)/shard_map/dot_general | solution.py:80
  191.9 3.4 scatter_custom_fusion
  195.3 8.6 %scatter_custom_fusion.1 = bf16[1152]{0:T(1024)(128)(2,1)S(1)} fusion(s32[768]{0:T(1024)S(1)} %fusion.55, bf16[768]{0:T(1024)(128)(2,1)S(1)} %broadcast.90, bf16[]{:T(256)} %constant.43.clone.1), kind=kCustom, calls=%fused_computation.92 | custom fusion | bytes 2306 | tf_op jit(solution)/shard_map/scatter | solution.py:100
  204.2 27.0 %reduce-scatter.2.cloned.1.call-done = bf16[128,2560]{1,0:T(8,128)(2,1)} async-done(((bf16[1024,2560]{1,0:T(8,128)(2,1)}), bf16[128,2560]{1,0:T(8,128)(2,1)}) %reduce-scatter.2.cloned.1.call-update) | async-done | bytes 655376 | tf_op jit(solution)/shard_map/reduce_scatter | solution.py:79
  231.3 1.4 fusion.37
  232.7 1.3 fusion.39
  234.0 6.3 %gather_fusion = bf16[1152,2560]{1,0:T(8,128)(2,1)} fusion(bf16[128,2560]{1,0:T(8,128)(2,1)S(1)} %fusion.39, s32[2048]{0:T(1024)S(1)} %pad_clamp_fusion), kind=kCustom, calls=%fused_computation | custom fusion | bytes 11801088 | tf_op jit(solution)/shard_map/gather | solution.py:101
  240.3 9.0 %gather.9 = bf16[128,9,2560]{2,1,0:T(8,128)(2,1)} reshape(bf16[1152,2560]{1,0:T(8,128)(2,1)} %gather_fusion) | data formatting | bytes 11796480 | tf_op jit(solution)/shard_map/gather | solution.py:101
  249.3 5.6 broadcast_multiply_fusion
  254.9 126.6 %all_to_all.26 = bf16[128,9,2560]{2,1,0:T(8,128)(2,1)} all-to-all(bf16[128,9,2560]{2,1,0:T(8,128)(2,1)S(1)} %broadcast_multiply_fusion), channel_id=1, replica_groups=mesh['ctx'=8,'exp'=16] {'ctx','exp'}, dimensions={0} | all-to-all | bytes 11796480 | tf_op jit(solution)/shard_map/all_to_all | solution.py:102
  381.6 9.5 %reshape.99 = bf16[1152,2560]{1,0:T(8,128)(2,1)} reshape(bf16[128,9,2560]{2,1,0:T(8,128)(2,1)} %all_to_all.26) | data formatting | bytes 11796480 | tf_op jit(solution)/shard_map/reshape | solution.py:103
  391.1 10.4 %fusion.31 = f32[1152,768]{1,0:T(8,128)} fusion(bf16[1152,2560]{1,0:T(8,128)(2,1)} %reshape.99, bf16[1,2560,768]{2,1,0:T(8,128)(2,1)} %param.27), kind=kOutput, calls=%fused_computation.52 | convolution fusion | flops 4529848320 | bytes 13369344 | tf_op jit(solution)/shard_map/dot_general | solution.py:104
  401.5 18.8 %convolution_convert_fusion.2 = bf16[1152,2560]{1,0:T(8,128)(2,1)} fusion(bf16[1,768,2560]{2,1,0:T(8,128)(2,1)} %param.29, bf16[1152,2560]{1,0:T(8,128)(2,1)} %reshape.99, bf16[1,2560,768]{2,1,0:T(8,128)(2,1)} %param.28, f32[1152,768]{1,0:T(8,128)} %fusion.31), kind=kOutput, calls=%fused_computation.45 | convolution fusion | flops 9067954176 | bytes 23199744 | tf_op jit(solution)/shard_map/dot_general | solution.py:107
  420.3 9.0 %reshape.100 = bf16[128,9,2560]{2,1,0:T(8,128)(2,1)} reshape(bf16[1152,2560]{1,0:T(8,128)(2,1)} %convolution_convert_fusion.2) | data formatting | bytes 11796480 | tf_op jit(solution)/shard_map/reshape | solution.py:109
  429.3 7.2 %all-to-all-start.2 = ((bf16[128,9,2560]{2,1,0:T(8,128)(2,1)}), bf16[128,9,2560]{2,1,0:T(8,128)(2,1)}, u32[]{:S(2)}, u32[]{:S(2)}) async-start(bf16[128,9,2560]{2,1,0:T(8,128)(2,1)} %reshape.100), calls=%async_computation.3 | async-start | bytes 20971520 | tf_op jit(solution)/shard_map/all_to_all | solution.py:108
  436.6 140.7 %all-to-all-done.2 = bf16[128,9,2560]{2,1,0:T(8,128)(2,1)} async-done(((bf16[128,9,2560]{2,1,0:T(8,128)(2,1)}), bf16[128,9,2560]{2,1,0:T(8,128)(2,1)}, u32[]{:S(2)}, u32[]{:S(2)}) %all-to-all-start.2) | async-done | bytes 5898272 | tf_op jit(solution)/shard_map/all_to_all | solution.py:108
  577.3 9.5 %reshape.101 = bf16[1152,2560]{1,0:T(8,128)(2,1)} reshape(bf16[128,9,2560]{2,1,0:T(8,128)(2,1)} %all-to-all-done.2) | data formatting | bytes 11796480 | tf_op jit(solution)/shard_map/reshape | solution.py:111
  586.9 11.8 %gather_fusion.1 = bf16[768,2560]{1,0:T(8,128)(2,1)} fusion(bf16[1152,2560]{1,0:T(8,128)(2,1)} %reshape.101, s32[1024]{0:T(1024)S(1)} %pad_clamp_fusion.1), kind=kCustom, calls=%fused_computation.1 | custom fusion | bytes 7867392 | tf_op jit(solution)/shard_map/gather | solution.py:111
  598.7 7.7 %reshape.103 = f32[128,6,2560]{2,1,0:T(8,128)} reshape(bf16[768,2560]{1,0:T(8,128)(2,1)} %gather_fusion.1) | data formatting | bytes 11796480 | tf_op jit(solution)/shard_map/convert_element_type | solution.py:114
  606.4 8.0 %multiply_reduce_fusion = f32[128,2560]{1,0:T(8,128)S(1)} fusion(f32[128,6,2560]{2,1,0:T(8,128)} %reshape.103, f32[128,6]{1,0:T(8,128)S(1)} %bitcast.103), kind=kLoop, calls=%fused_computation.46 | loop fusion | flops 3604480 | bytes 9178112 | tf_op jit(solution)/shard_map/reduce_sum | solution.py:114
  (113 shorter events, 36.0 us)
Async XLA Ops:
  6.5 58.8 %copy-start = (bf16[512,1024]{1,0:T(8,128)(2,1)S(1)}, bf16[512,1024]{1,0:T(8,128)(2,1)}, u32[]{:S(2)}) copy-start(bf16[512,1024]{1,0:T(8,128)(2,1)} %param.21) | copy-start | bytes 3145732
  11.3 5.4 copy-start.4
  11.3 72.3 %all-to-all-start = ((bf16[128,8,1536]{0,2,1:T(8,128)(2,1)}), bf16[128,8,1536]{0,2,1:T(8,128)(2,1)}, u32[]{:S(2)}, u32[]{:S(2)}) async-start(bf16[128,8,1536]{0,2,1:T(8,128)(2,1)} %bitcast.93), calls=%async_computation | async-start | bytes 6291456 | tf_op jit(solution)/shard_map/all_to_all | solution.py:35
  15.9 49.4 %all-gather.4.cloned.1.call-start = ((), (), s32[]{:S(2)}) async-start(), calls=%async_computation.5 | async-start | bytes 1179648 | tf_op jit(solution)/shard_map/all_gather | solution.py:37
  16.7 214.6 %reduce-scatter.2.cloned.1.call-start = ((), (), s32[]{:S(2)}) async-start(), calls=%async_computation.4 | async-start | bytes 5898240 | tf_op jit(solution)/shard_map/reduce_scatter | solution.py:79
  69.2 4.2 copy-start.8
  190.3 0.7 copy-start.6
  190.3 41.0 %copy-start.2 = (bf16[1,128,2560]{2,1,0:T(8,128)(2,1)S(1)}, bf16[1,128,2560]{2,1,0:T(8,128)(2,1)}, u32[]{:S(2)}) copy-start(bf16[1,128,2560]{2,1,0:T(8,128)(2,1)} %param.17) | copy-start | bytes 1966084
  190.3 42.4 %copy-start.5 = (f32[2560]{0:T(1024)S(1)}, f32[2560]{0:T(1024)}, u32[]{:S(2)}) copy-start(f32[2560]{0:T(1024)} %param.24) | copy-start | bytes 30724
  429.3 7.2 %copy-start.7 = (f32[1,128,6]{1,0,2:T(1,128)S(1)}, f32[1,128,6]{1,0,2:T(1,128)}, u32[]{:S(2)}) copy-start(f32[1,128,6]{1,0,2:T(1,128)} %param.26) | copy-start | bytes 9220
  429.3 148.0 %all-to-all-start.2 = ((bf16[128,9,2560]{2,1,0:T(8,128)(2,1)}), bf16[128,9,2560]{2,1,0:T(8,128)(2,1)}, u32[]{:S(2)}, u32[]{:S(2)}) async-start(bf16[128,9,2560]{2,1,0:T(8,128)(2,1)} %reshape.100), calls=%async_computation.3 | async-start | bytes 20971520 | tf_op jit(solution)/shard_map/all_to_all | solution.py:108
  606.4 8.0 %copy-start.3 = (bf16[128,2560]{1,0:T(8,128)(2,1)S(1)}, bf16[128,2560]{1,0:T(8,128)(2,1)}, u32[]{:S(2)}) copy-start(bf16[128,2560]{1,0:T(8,128)(2,1)} %reduce-scatter.2.cloned.1.call-done) | copy-start | bytes 1966084
  606.4 9.1 %copy-start.1 = (bf16[512,1024]{1,0:T(8,128)(2,1)S(1)}, bf16[512,1024]{1,0:T(8,128)(2,1)}, u32[]{:S(2)}) copy-start(bf16[512,1024]{1,0:T(8,128)(2,1)} %param.21) | copy-start | bytes 3145732
Sparse Core Ops, SparseCore 0:
  18.5 28.5 all-gather.3
  190.4 40.7 reduce-scatter.1
where the time goes:
time: 634 us; the launch traced here: 623 us
  blocking collectives  174 us (27%)
  waiting for transfers between devices  168 us (26%)
  local copies, waits for them, and re-layouts  135 us (21%)
  matrix products  93.8 us (15%)
  other arithmetic  25 us (4%)
  between operations  14 us (2%)
  starting transfers between devices  11.9 us (2%)
    all_to_all x1, waiting for transfers between devices, local(): lax.all_to_all(result.reshape(arrived.shape), ('ctx', 'exp'), split_axis=...  141 us
    all_to_all x1, blocking collectives, local(): lax.all_to_all(outgoing, ('ctx', 'exp'), split_axis=0, concat_axis=0, til...  127 us
    all_gather x1, blocking collectives, local(): lax.all_gather(key_rope[0], 'ctx', axis=0, tiled=True)  47.8 us
    reduce_scatter x1, waiting for transfers between devices, local(): lax.psum_scatter(jnp.dot(mixed_heads, w_o, preferred_element_type=jnp.flo...  27 us
    dot_general x16, matrix products, one_head(): jnp.dot(one_query, key_full.T, preferred_element_type=jnp.float32)  24.1 us
    dot_general x16, matrix products, one_head(): jnp.dot(weights, one_value, preferred_element_type=jnp.float32)  22.2 us
    dot_general x1, matrix products, local(): jnp.dot(active, w_down[0], preferred_element_type=jnp.float32)  18.8 us
    gather x2, local copies, waits for them, and re-layouts, local(): normed[source_row] * filled[:, None]  15.3 us
  transfers between devices with their start and end apart: 4, of which 2 were waited for; matrix products, arithmetic and copies ran while one was open for 5% of the time, Pallas kernels for 0%

commit v1 on v0

v1 whole, which is shorter than its diff:
```python
import functools
import math

import jax
import jax.numpy as jnp
from jax import lax
from jax.experimental import pallas as pl
from jax.experimental.pallas import tpu as pltpu
from jax.sharding import PartitionSpec as P

NOPE = 128
ROPE = 64
VDIM = 128
KVL = 512
D = 2560
FF = 768
TOPK = 6
CAP = 9
TOK = 128
LEN = 1024
QW = 1536
RING = 4
ROWS = 72
CHUNKS = 5
CW = 256
HALF = 1280
CHIP = 256
LATW = 640
MESH = pl.DeviceIdType.MESH
BF = jnp.bfloat16
F32 = jnp.float32
ANY = pl.BlockSpec(memory_space=pl.ANY)
VM = pl.BlockSpec(memory_space=pltpu.VMEM)
DMA = pltpu.SemaphoreType.DMA


def place():
    c = lax.axis_index("ctx")
    e = lax.axis_index("exp")
    return c // 2, c % 2, e // RING, e % RING


def device(y, core, z, x):
    return (y * 2 + core, z * RING + x)


def step(v, d):
    return lax.rem(v + d, RING)


def remote(src, dst, send, recv, target):
    return pltpu.make_async_remote_copy(
        src_ref=src, dst_ref=dst, send_sem=send, recv_sem=recv, device_id=target, device_id_type=MESH
    )


def greet(targets):
    barrier = pltpu.get_barrier_semaphore()
    for target in targets:
        pl.semaphore_signal(barrier, inc=1, device_id=target, device_id_type=MESH)
    pl.semaphore_wait(barrier, len(targets))


def attention_kernel(
    q_hbm, lat_hbm, uk_ref, uv_ref, out_ref, qbuf, lat, kbuf, vbuf, q_send, q_recv, l_send, l_recv, own_sem
):
    y, core, z, x = place()
    me = y * 2 + core
    peers = [(dy, dc) for dy in (0, 1, 3, 2) for dc in (0, 1) if (dy, dc) != (0, 0)]
    greet([device(step(y, dy), lax.rem(core + dc, 2), z, x) for dy, dc in peers])

    def lat_copy(dy, dc):
        i = dy * 2 + dc
        target = device(step(y, dy), lax.rem(core + dc, 2), z, x)
        return remote(lat_hbm, lat.at[me], l_send.at[i], l_recv.at[i], target)

    def q_copy(dy, dc):
        i = dy * 2 + dc
        yy, cc = step(y, dy), lax.rem(core + dc, 2)
        columns = pl.ds(pl.multiple_of((yy * 2 + cc) * QW, 128), QW)
        return remote(q_hbm.at[:, columns], qbuf.at[me], q_send.at[i], q_recv.at[i], device(yy, cc, z, x))

    own_lat = pltpu.make_async_copy(lat_hbm, lat.at[me], own_sem.at[0])
    own_q = pltpu.make_async_copy(
        q_hbm.at[:, pl.ds(pl.multiple_of(me * QW, 128), QW)], qbuf.at[me], own_sem.at[1]
    )
    own_lat.start()
    own_q.start()
    for dy, dc in peers:
        lat_copy(dy, dc).start()
    for dy, dc in peers:
        q_copy(dy, dc).start()
    own_lat.wait()
    own_q.wait()
    for dy, dc in peers:
        lat_copy(dy, dc).wait()

    lane = lax.broadcasted_iota(jnp.int32, (CHIP, 128), 1)

    def project(b, carry):
        rows = pl.ds(pl.multiple_of(b * CHIP, CHIP), CHIP)
        block = lat[pl.ds(b * 2, 2)].reshape(CHIP, LATW)
        latent = block[:, :KVL]
        rope = block[:, KVL:].astype(F32)
        rope_low = jnp.where(lane < 64, rope, 0.0).astype(BF)
        rope_high = pltpu.roll(rope, 64, 1)
        for h in range(8):
            nope = jnp.dot(latent, uk_ref[:, h * 128 : h * 128 + 128], preferred_element_type=F32)
            if h % 2 == 0:
                kbuf[h, rows, 0:128] = nope.astype(BF)
                kbuf[h, rows, 128:256] = rope_low
            else:
                turned = pltpu.roll(nope, 64, 1)
                kbuf[h, rows, 0:128] = jnp.where(lane < 64, 0.0, turned).astype(BF)
                kbuf[h, rows, 128:256] = jnp.where(lane < 64, turned, rope_high).astype(BF)
        vbuf[rows, :] = jnp.dot(latent, uv_ref[...], preferred_element_type=F32).astype(BF)
        return carry

    lax.fori_loop(0, RING, project, 0)

    factor = 1.0 / math.sqrt(NOPE + ROPE) * math.log2(math.e)
    row_at = lax.broadcasted_iota(jnp.int32, (CHIP, CHIP), 0)
    col_at = lax.broadcasted_iota(jnp.int32, (CHIP, CHIP), 1)
    causal = row_at >= col_at

    def attend(block):
        length = (block + 1) * CHIP

        def pair(p, carry):
            columns = pl.ds(pl.multiple_of(p * 384, 128), 384)
            q = qbuf[block * 2 : block * 2 + 2, :, columns].reshape(CHIP, 384)
            outs = []
            for odd in range(2):
                query = q[:, odd * 128 : odd * 128 + 256]
                head = p * 2 + odd
                contract = (((1,), (1,)), ((), ()))
                last = lax.dot_general(
                    query, kbuf[head, length - CHIP : length], contract, preferred_element_type=F32
                )
                last = jnp.where(causal, last, -jnp.inf)
                peak = jnp.max(last, axis=1, keepdims=True)
                if block:
                    first = lax.dot_general(
                        query, kbuf[head, 0 : length - CHIP], contract, preferred_element_type=F32
                    )
                    peak = jnp.maximum(peak, jnp.max(first, axis=1, keepdims=True))
                values = pl.ds(pl.multiple_of(head * 128, 128), 128)
                weight = jnp.exp2((last - peak) * factor)
                total = jnp.sum(weight, axis=1, keepdims=True)
                result = jnp.dot(
                    weight.astype(BF), vbuf[length - CHIP : length, values], preferred_element_type=F32
                )
                if block:
                    weight = jnp.exp2((first - peak) * factor)
                    total += jnp.sum(weight, axis=1, keepdims=True)
                    result += jnp.dot(
                        weight.astype(BF), vbuf[0 : length - CHIP, values], preferred_element_type=F32
                    )
                outs.append((result / total).astype(BF))
            out_ref[block * CHIP : (block + 1) * CHIP, pl.ds(pl.multiple_of(p * 256, 256), 256)] = (
                jnp.concatenate(outs, axis=1)
            )
            return carry

        lax.fori_loop(0, 4, pair, 0)

    for dy in (0, 1, 3, 2):
        for dc in range(2):
            if (dy, dc) != (0, 0):
                q_copy((4 - dy) % 4, dc).wait_recv()
        source = lax.rem(y + dy, RING)
        for block in range(RING):
            pl.when(source == block)(functools.partial(attend, block))
    for dy, dc in peers:
        q_copy(dy, dc).wait_send()


def attention_call(queries, latrope, w_uk, w_uv):
    return pl.pallas_call(
        attention_kernel,
        out_shape=jax.ShapeDtypeStruct((LEN, 1024), BF),
        in_specs=[ANY, ANY, VM, VM],
        out_specs=VM,
        scratch_shapes=[
            pltpu.VMEM((8, TOK, QW), BF),
            pltpu.VMEM((8, TOK, LATW), BF),
            pltpu.VMEM((8, LEN, 256), BF),
            pltpu.VMEM((LEN, 1024), BF),
            DMA((8,)),
            DMA((8,)),
            DMA((8,)),
            DMA((8,)),
            DMA((2,)),
        ],
        compiler_params=pltpu.CompilerParams(
            collective_id=1, has_side_effects=True, vmem_limit_bytes=48 * 2**20
        ),
        name="attention",
    )(queries, latrope, w_uk, w_uv)


def exp_targets(y, core, z, x):
    found = [device(y, 1 - core, z, x)]
    for d in (1, 2, 3):
        found.append(device(step(y, d), core, z, x))
        found.append(device(y, core, step(z, d), x))
        found.append(device(y, core, z, step(x, d)))
    return found


def first_phase(j, spot, src, mid, send, recv, own):
    y, core, z, x = spot
    copies = []
    for d in (1, 3, 2):
        xx, zz = step(x, d), step(z, d)
        copies.append(
            remote(src.at[j, 0, :, xx], mid.at[j, 0, x], send.at[j, d], recv.at[j, d], device(y, core, z, xx))
        )
        copies.append(
            remote(
                src.at[j, 1, zz], mid.at[j, 1, z], send.at[j, 3 + d], recv.at[j, 3 + d], device(y, core, zz, x)
            )
        )
    copies.append(pltpu.make_async_copy(src.at[j, 0, :, x], mid.at[j, 0, x], own.at[j, 0]))
    copies.append(pltpu.make_async_copy(src.at[j, 1, z], mid.at[j, 1, z], own.at[j, 1]))
    return copies


def second_phase(j, spot, mid, dst, send, recv, own):
    y, core, z, x = spot
    copies = []
    for d in (1, 3, 2):
        xx, zz = step(x, d), step(z, d)
        copies.append(
            remote(mid.at[j, 0, :, zz], dst.at[j, 0, z], send.at[j, d], recv.at[j, d], device(y, core, zz, x))
        )
        copies.append(
            remote(
                mid.at[j, 1, :, xx],
                dst.at[j, 1, :, x],
                send.at[j, 3 + d],
                recv.at[j, 3 + d],
                device(y, core, z, xx),
            )
        )
    copies.append(pltpu.make_async_copy(mid.at[j, 0, :, z], dst.at[j, 0, z], own.at[j, 0]))
    copies.append(pltpu.make_async_copy(mid.at[j, 1, :, x], dst.at[j, 1, :, x], own.at[j, 1]))
    return copies


def pipeline(stages):
    depth = len(stages)

    def turn(t, carry):
        for at in range(depth - 1, -1, -1):
            j = t - at

            @pl.when((j >= 0) & (j < CHUNKS))
            def _(at=at, j=j):
                stages[at](j)

        return carry

    lax.fori_loop(0, CHUNKS + depth - 1, turn, 0)


def start_all(copies):
    for copy in copies:
        copy.start()


def wait_all(copies):
    for copy in copies:
        copy.wait()


def dispatch_kernel(
    mixed_hbm, wo_hbm, stream_hbm, gm_ref, x_out, hown_ref,
    mixed, wo, p_own, p_sib, r_core, rs_buf, hbuf, gs, t1, sx,
    in_sem, wo_sem, st_sem, c1_s, c1_r, rs_s, rs_r, ag_s, ag_r, c2_s, c2_r, p1_s, p1_r, p2_s, p2_r, o1, o2,
):
    spot = place()
    y, core, z, x = spot
    sibling = device(y, 1 - core, z, x)

    def columns(half, j):
        return pl.ds(pl.multiple_of(half * HALF + j * CW, 128), CW)

    def wo_copy(j, side):
        half = core if side == 0 else 1 - core
        return pltpu.make_async_copy(wo_hbm.at[:, columns(half, j)], wo.at[j, side], wo_sem.at[j, side])

    def half_of(which):
        return pl.ds(pl.multiple_of(which * HALF, 128), HALF)

    mixed_copy = pltpu.make_async_copy(mixed_hbm, mixed, in_sem.at[0])
    stream_copy = pltpu.make_async_copy(stream_hbm.at[:, half_of(core)], sx.at[core], in_sem.at[1])
    mixed_copy.start()
    stream_copy.start()
    for j in range(CHUNKS):
        for side in range(2):
            wo_copy(j, side).start()
    greet(exp_targets(y, core, z, x))
    stream_send = remote(
        stream_hbm.at[:, half_of(1 - core)], sx.at[core], st_sem.at[0], st_sem.at[1], sibling
    )
    stream_send.start()
    mixed_copy.wait()
    stream_copy.wait()

    def core_sum(j):
        return remote(p_sib.at[j], r_core.at[j], c1_s.at[j], c1_r.at[j], sibling)

    def rows_of(which):
        return pl.ds(pl.multiple_of(which * CHIP, CHIP), CHIP)

    def scatter(j):
        return [
            remote(
                p_own.at[j, rows_of(step(y, d))],
                rs_buf.at[j, d - 1],
                rs_s.at[j, d],
                rs_r.at[j, d],
                device(step(y, d), core, z, x),
            )
            for d in (1, 3, 2)
        ]

    def spread(j):
        return [
            remote(
                hbuf.at[j, core, rows_of(y)],
                hbuf.at[j, core, rows_of(y)],
                ag_s.at[j, d],
                ag_r.at[j, d],
                device(step(y, d), core, z, x),
            )
            for d in (1, 3, 2)
        ]

    def core_share(j):
        return remote(hbuf.at[j, core], hbuf.at[j, core], c2_s.at[j], c2_r.at[j], sibling)

    def one(j):
        return first_phase(j, spot, gs, t1, p1_s, p1_r, o1)

    def two(j):
        return second_phase(j, spot, t1, x_out, p2_s, p2_r, o2)

    def project(j):
        for side in range(2):
            wo_copy(j, side).wait()

        def block(b, carry):
            rows = rows_of(b)
            left = mixed[rows, :]
            p_sib[j, rows] = jnp.dot(left, wo[j, 1], preferred_element_type=F32).astype(BF)
            p_own[j, rows] = jnp.dot(left, wo[j, 0], preferred_element_type=F32).astype(BF)
            return carry

        lax.fori_loop(0, RING, block, 0)
        core_sum(j).start()

    def add_core(j):
        core_sum(j).wait()
        p_own[j] = (p_own[j].astype(F32) + r_core[j].astype(F32)).astype(BF)
        start_all(scatter(j))

    def finish_hidden(j):
        wait_all(scatter(j))
        total = p_own[j, rows_of(y)].astype(F32)
        for i in range(3):
            total += rs_buf[j, i].astype(F32)
        stream = sx[:, :, pl.ds(pl.multiple_of(j * CW, 128), CW)].reshape(CHIP, CW)
        hidden = (stream.astype(F32) + total).astype(BF)
        hbuf[j, core, rows_of(y)] = hidden
        hown_ref[j] = hidden
        start_all(spread(j))

    def share(j):
        wait_all(spread(j))
        core_share(j).start()

    def pick(j):
        core_share(j).wait()

        def block(b, carry):
            left = gm_ref[pl.ds(pl.multiple_of(b * 288, 16), 288), :]
            for half in range(2):
                picked = jnp.dot(left, hbuf[j, half], preferred_element_type=F32)
                gs[j, half, b] = picked.reshape(RING, ROWS, CW).astype(BF)
            return carry

        lax.fori_loop(0, RING, block, 0)
        start_all(one(j))

    def forward(j):
        wait_all(one(j))
        start_all(two(j))

    def drain(j, carry):
        wait_all(two(j))
        return carry

    stream_send.wait()
    pipeline([project, add_core, finish_hidden, share, pick, forward])
    lax.fori_loop(0, CHUNKS, drain, 0)


def dispatch_call(mixed, w_o, stream, gm):
    grid_rows = (CHUNKS, 2, RING, RING, ROWS, CW)
    return pl.pallas_call(
        dispatch_kernel,
        out_shape=(jax.ShapeDtypeStruct(grid_rows, BF), jax.ShapeDtypeStruct((CHUNKS, CHIP, CW), BF)),
        in_specs=[ANY, ANY, ANY, VM],
        out_specs=(ANY, VM),
        scratch_shapes=[
            pltpu.VMEM((LEN, 1024), BF),
            pltpu.VMEM((CHUNKS, 2, 1024, CW), BF),
            pltpu.VMEM((CHUNKS, LEN, CW), BF),
            pltpu.VMEM((CHUNKS, LEN, CW), BF),
            pltpu.VMEM((CHUNKS, LEN, CW), BF),
            pltpu.VMEM((CHUNKS, 3, CHIP, CW), BF),
            pltpu.VMEM((CHUNKS, 2, LEN, CW), BF),
            pltpu.VMEM(grid_rows, BF),
            pltpu.VMEM(grid_rows, BF),
            pltpu.VMEM((2, TOK, HALF), BF),
            DMA((2,)),
            DMA((CHUNKS, 2)),
            DMA((2,)),
            DMA((CHUNKS,)),
            DMA((CHUNKS,)),
            DMA((CHUNKS, 4)),
            DMA((CHUNKS, 4)),
            DMA((CHUNKS, 4)),
            DMA((CHUNKS, 4)),
            DMA((CHUNKS,)),
            DMA((CHUNKS,)),
            DMA((CHUNKS, 7)),
            DMA((CHUNKS, 7)),
            DMA((CHUNKS, 7)),
            DMA((CHUNKS, 7)),
            DMA((CHUNKS, 2)),
            DMA((CHUNKS, 2)),
        ],
        compiler_params=pltpu.CompilerParams(
            collective_id=2, has_side_effects=True, vmem_limit_bytes=60 * 2**20
        ),
        name="dispatch",
    )(mixed, w_o, stream, gm)


def expert_kernel(
    x_hbm, wg_hbm, wu_hbm, wd_hbm, gain_ref, wc_hbm, hown_ref, out_ref,
    xbuf, wg, wu, wd, act, t1, back, wc, p_own, p_sib, r_core, rs_buf, swap,
    in_sem, w_sem, c1_s, c1_r, rs_s, rs_r, sw_s, sw_r, p1_s, p1_r, p2_s, p2_r, o1, o2,
):
    spot = place()
    y, core, z, x = spot
    sibling = device(y, 1 - core, z, x)
    loads = [
        pltpu.make_async_copy(x_hbm, xbuf, in_sem.at[0]),
        pltpu.make_async_copy(wg_hbm, wg, w_sem.at[0]),
        pltpu.make_async_copy(wu_hbm, wu, w_sem.at[1]),
    ]
    later = [
        pltpu.make_async_copy(wd_hbm, wd, w_sem.at[2]),
        pltpu.make_async_copy(wc_hbm, wc, in_sem.at[1]),
    ]
    start_all(loads)
    start_all(later)
    greet(exp_targets(y, core, z, x))
    wait_all(loads)

    def rows_of(which):
        return pl.ds(pl.multiple_of(which * CHIP, CHIP), CHIP)

    def hidden_units(b, carry):
        squares = jnp.zeros((288, 1), F32)
        for j in range(CHUNKS):
            for half in range(2):
                part = xbuf[j, half, b].astype(F32).reshape(288, CW)
                squares += jnp.sum(part * part, axis=1, keepdims=True)
        scale = lax.rsqrt(squares * (1.0 / D) + 1e-06)
        gate = jnp.zeros((288, FF), F32)
        up = jnp.zeros((288, FF), F32)
        for half in range(2):
            parts = []
            for j in range(CHUNKS):
                at = half * HALF + j * CW
                part = xbuf[j, half, b].astype(F32).reshape(288, CW)
                parts.append((part * scale * gain_ref[:, at : at + CW]).astype(BF))
            left = jnp.concatenate(parts, axis=1)
            gate += jnp.dot(left, wg[half * HALF : (half + 1) * HALF], preferred_element_type=F32)
            up += jnp.dot(left, wu[half * HALF : (half + 1) * HALF], preferred_element_type=F32)
        act[pl.ds(pl.multiple_of(b * 288, 16), 288), :] = (gate / (1.0 + jnp.exp(-gate)) * up).astype(BF)
        return carry

    lax.fori_loop(0, RING, hidden_units, 0)
    wait_all(later)

    def one(j):
        return first_phase(j, spot, xbuf, t1, p1_s, p1_r, o1)

    def two(j):
        return second_phase(j, spot, t1, back, p2_s, p2_r, o2)

    def core_sum(j):
        return remote(p_sib.at[j], r_core.at[j], c1_s.at[j], c1_r.at[j], sibling)

    def scatter(j):
        return [
            remote(
                p_own.at[j, rows_of(step(y, d))],
                rs_buf.at[j, d - 1],
                rs_s.at[j, d],
                rs_r.at[j, d],
                device(step(y, d), core, z, x),
            )
            for d in (1, 3, 2)
        ]

    def exchange(j):
        return remote(swap.at[j, 1], swap.at[j, 2], sw_s.at[j], sw_r.at[j], sibling)

    def columns(half, j):
        return pl.ds(pl.multiple_of(half * HALF + j * CW, 128), CW)

    def down(j):
        def block(b, carry):
            left = act[pl.ds(pl.multiple_of(b * 288, 16), 288), :]
            for half in range(2):
                result = jnp.dot(left, wd[:, columns(half, j)], preferred_element_type=F32)
                xbuf[j, half, b] = result.reshape(RING, ROWS, CW).astype(BF)
            return carry

        lax.fori_loop(0, RING, block, 0)
        start_all(one(j))

    def forward(j):
        wait_all(one(j))
        start_all(two(j))

    def combine(j):
        wait_all(two(j))
        own = back[j, core].reshape(1152, CW)
        other = back[j, 1 - core].reshape(1152, CW)

        def block(b, carry):
            rows = rows_of(b)
            left = wc[rows, :]
            p_sib[j, rows] = jnp.dot(left, other, preferred_element_type=F32).astype(BF)
            p_own[j, rows] = jnp.dot(left, own, preferred_element_type=F32).astype(BF)
            return carry

        lax.fori_loop(0, RING, block, 0)
        core_sum(j).start()

    def add_core(j):
        core_sum(j).wait()
        p_own[j] = (p_own[j].astype(F32) + r_core[j].astype(F32)).astype(BF)
        start_all(scatter(j))

    def finish(j):
        wait_all(scatter(j))
        total = p_own[j, rows_of(y)].astype(F32)
        for i in range(3):
            total += rs_buf[j, i].astype(F32)
        total = (hown_ref[j].astype(F32) + total).astype(BF)
        mine = jnp.where(core == 0, total[:TOK], total[TOK:])
        theirs = jnp.where(core == 0, total[TOK:], total[:TOK])
        swap[j, 1] = theirs
        exchange(j).start()
        out_ref[:, columns(core, j)] = mine

    def land(j):
        exchange(j).wait()
        out_ref[:, columns(1 - core, j)] = swap[j, 2]

    pipeline([down, forward, combine, add_core, finish, land])


def expert_call(x, w_gate, w_up, w_down, gain, wc, hown):
    grid_rows = (CHUNKS, 2, RING, RING, ROWS, CW)
    return pl.pallas_call(
        expert_kernel,
        out_shape=jax.ShapeDtypeStruct((TOK, D), BF),
        in_specs=[ANY, ANY, ANY, ANY, VM, ANY, VM],
        out_specs=VM,
        scratch_shapes=[
            pltpu.VMEM(grid_rows, BF),
            pltpu.VMEM((D, FF), BF),
            pltpu.VMEM((D, FF), BF),
            pltpu.VMEM((FF, D), BF),
            pltpu.VMEM((1152, FF), BF),
            pltpu.VMEM(grid_rows, BF),
            pltpu.VMEM(grid_rows, BF),
            pltpu.VMEM((LEN, 1152), BF),
            pltpu.VMEM((CHUNKS, LEN, CW), BF),
            pltpu.VMEM((CHUNKS, LEN, CW), BF),
            pltpu.VMEM((CHUNKS, LEN, CW), BF),
            pltpu.VMEM((CHUNKS, 3, CHIP, CW), BF),
            pltpu.VMEM((CHUNKS, 3, TOK, CW), BF),
            DMA((2,)),
            DMA((3,)),
            DMA((CHUNKS,)),
            DMA((CHUNKS,)),
            DMA((CHUNKS, 4)),
            DMA((CHUNKS, 4)),
            DMA((CHUNKS,)),
            DMA((CHUNKS,)),
            DMA((CHUNKS, 7)),
            DMA((CHUNKS, 7)),
            DMA((CHUNKS, 7)),
            DMA((CHUNKS, 7)),
            DMA((CHUNKS, 2)),
            DMA((CHUNKS, 2)),
        ],
        compiler_params=pltpu.CompilerParams(
            collective_id=3, has_side_effects=True, vmem_limit_bytes=62 * 2**20
        ),
        name="experts",
    )(x, w_gate, w_up, w_down, gain, wc, hown)


def routing(expert_ids, gate_weights):
    ids = lax.all_gather(expert_ids, "ctx", axis=0, tiled=True)
    gates = lax.all_gather(gate_weights, "ctx", axis=0, tiled=True)
    first = lax.axis_index("ctx") * 16
    hit = ids[:, :, None] == (first + jnp.arange(16))[None, None, :]
    named = jnp.any(hit, axis=1)
    gate = jnp.sum(jnp.where(hit, gates[:, :, None], 0.0), axis=1)
    blocks = named.astype(BF).reshape(8, TOK, 16)
    earlier = (jnp.arange(TOK)[:, None] > jnp.arange(TOK)[None, :]).astype(BF)
    slot = jnp.einsum("ij,bje->bie", earlier, blocks, preferred_element_type=F32)
    spot = jnp.arange(8, dtype=F32)[:, None, None] * CAP + slot
    spot = jnp.where(named, spot.reshape(LEN, 16), -1.0)
    rows = jnp.arange(ROWS, dtype=F32)
    gm = (spot.T[:, None, :] == rows[None, :, None]).astype(BF).reshape(1152, LEN)
    widen = (jnp.arange(16)[:, None] == (jnp.arange(1152) // ROWS)[None, :]).astype(BF)
    wide = jnp.dot(spot.astype(BF), widen, preferred_element_type=F32)
    gate_wide = jnp.dot(gate.astype(BF), widen, preferred_element_type=F32)
    at = (jnp.arange(1152) % ROWS).astype(F32)
    wc = jnp.where(wide == at[None, :], gate_wide, 0.0).astype(BF)
    return gm, wc


def local(
    stream_in,
    queries,
    latents,
    key_rope,
    w_uk,
    w_uv,
    w_o,
    norm_gain,
    expert_ids,
    gate_weights,
    w_gate,
    w_up,
    w_down,
):
    gm, wc = routing(expert_ids[0], gate_weights[0])
    latrope = jnp.concatenate([latents[0], key_rope[0], jnp.zeros((TOK, 64), BF)], axis=1)
    mixed = attention_call(queries[0], latrope, w_uk, w_uv)
    arrived, hown = dispatch_call(mixed, w_o, stream_in[0], gm)
    out = expert_call(arrived, w_gate[0], w_up[0], w_down[0], norm_gain[None, :], wc, hown)
    return out[None]


def solution(mesh):
    return jax.shard_map(
        local,
        mesh=mesh,
        in_specs=(
            P("exp", "ctx", None),
            P("exp", "ctx", None),
            P("exp", "ctx", None),
            P("exp", "ctx", None),
            P(None, "ctx"),
            P(None, "ctx"),
            P("ctx", None),
            P(),
            P("exp", "ctx", None),
            P("exp", "ctx", None),
            P(("ctx", "exp"), None, None),
            P(("ctx", "exp"), None, None),
            P(("ctx", "exp"), None, None),
        ),
        out_specs=P("exp", "ctx", None),
        check_vma=False,
    )
```

time: 634 us -> 315 us (0.50); the launches traced: 623 us -> 311 us
  Pallas kernels: 0 us -> 282 us
  waiting for transfers between devices: 168 us -> 0 us
  blocking collectives: 174 us -> 19.4 us
  local copies, waits for them, and re-layouts: 135 us -> 4.22 us
  matrix products: 93.8 us -> 3.17 us
  other arithmetic: 25 us -> 2.26 us
  between operations: 14 us -> 0.17 us
  starting transfers between devices: 11.9 us -> 0 us
    pallas_call x0 -> x3, Pallas kernels: none -> 282 us  [the longest x1 115 us: dispatch_call(): pl.pallas_call(dispatch_kernel, out_shape=(jax.ShapeDtypeStruct(grid_rows...]
    all_to_all x2 -> x0, waiting for transfers between devices: 141 us -> none  [the longest x1 141 us: local(): lax.all_to_all(result.reshape(arrived.shape), ('ctx', 'exp'), split_axis=...]
    all_to_all x1 -> x0, blocking collectives: 127 us -> none  [local(): lax.all_to_all(outgoing, ('ctx', 'exp'), split_axis=0, concat_axis=0, til...]
    dot_general x38 -> x3, matrix products: 93.8 us -> 3.17 us  [the longest x1 2.24 us: routing(): gate_wide = jnp.dot(gate.astype(BF), widen, preferred_element_type=F32)]
    reshape x6 -> x0, local copies, waits for them, and re-layouts: 40.9 us -> none  [the longest x1 9.55 us: local(): flat_rows = arrived.reshape(-1, model_width)]
    all_gather x1 -> x2, blocking collectives: 47.8 us -> 19.4 us  [the longest x1 11.2 us: routing(): ids = lax.all_gather(expert_ids, 'ctx', axis=0, tiled=True)]
    gather x3 -> x0, local copies, waits for them, and re-layouts: 27.1 us -> none  [the longest x2 15.3 us: local(): normed[source_row] * filled[:, None]]
    reduce_scatter x1 -> x0, waiting for transfers between devices: 27 us -> none  [local(): lax.psum_scatter(jnp.dot(mixed_heads, w_o, preferred_element_type=jnp.flo...]
  transfers between devices with their start and end apart: 4 -> 0, of which waited for: 2 -> 0; matrix products, arithmetic and copies ran while one was open for 5% -> 0% of each run, Pallas kernels for 0% -> 0%
where the time goes in v1:
time: 315 us; the launch traced here: 311 us
  Pallas kernels  282 us (90%)
  blocking collectives  19.4 us (6%)
  local copies, waits for them, and re-layouts  4.22 us (1%)
  matrix products  3.17 us (1%)
    pallas_call x1, Pallas kernels, dispatch_call(): pl.pallas_call(dispatch_kernel, out_shape=(jax.ShapeDtypeStruct(grid_rows...  115 us
    pallas_call x1, Pallas kernels, expert_call(): pl.pallas_call(expert_kernel, out_shape=jax.ShapeDtypeStruct((TOK, D), BF...  110 us
    pallas_call x1, Pallas kernels, attention_call(): pl.pallas_call(attention_kernel, out_shape=jax.ShapeDtypeStruct((LEN, 102...  56.9 us
    all_gather x1, blocking collectives, routing(): ids = lax.all_gather(expert_ids, 'ctx', axis=0, tiled=True)  11.2 us
    all_gather x1, blocking collectives, routing(): gates = lax.all_gather(gate_weights, 'ctx', axis=0, tiled=True)  8.2 us

profile of v1, /device:TPU:34, one launch (start us, length us, event | category | flops | bytes accessed | tf_op | source)
XLA Modules:
  0.0 311.5 jit_solution(7696494823784349357)
XLA Ops:
  0.0 0.0 copy-start.6
  0.0 11.2 %all-gather = s32[1,1024,6]{1,0,2:T(1,128)S(1)} all-gather(s32[1,128,6]{1,0,2:T(1,128)} %param.21), channel_id=2, replica_groups=mesh['ctx'=8,'exp'=16] {'ctx'}, dimensions={1}, use_global_device_ids=true | all-gather | bytes 27648 | tf_op jit(solution)/shard_map/all_gather | solution.py:627
  11.3 0.1 compare_reduce_fusion
  11.4 0.1 fusion.2
  11.5 0.1 add_select_fusion
  11.6 0.8 fusion.4
  12.4 0.0 copy-done.6
  12.4 8.2 %all-gather.1 = f32[1,1024,6]{1,0,2:T(1,128)S(1)} all-gather(f32[1,128,6]{1,0,2:T(1,128)S(1)} %copy-done.6), channel_id=3, replica_groups=mesh['ctx'=8,'exp'=16] {'ctx'}, dimensions={1}, use_global_device_ids=true | all-gather | bytes 27648 | tf_op jit(solution)/shard_map/all_gather | solution.py:628
  20.6 0.1 fusion.3
  20.7 0.0 copy-start.4
  20.7 0.0 copy-start.3
  20.7 0.0 copy-start.1
  20.7 0.0 copy-start.2
  20.8 2.2 fusion.1.wc_hbm
  23.0 0.1 eq.68
  23.1 1.9 fusion.gm_ref
  25.0 0.0 copy-done.4
  25.0 0.1 copy.22
  25.2 0.1 pad.2.clone
  25.2 0.0 copy-done.3
  25.3 0.0 copy-done.1
  25.3 0.0 copy-done.2
  25.3 56.9 %attention.1.mixed_hbm = bf16[1024,1024]{1,0:T(8,128)(2,1)S(1)} custom-call(bf16[128,12288]{1,0:T(8,128)(2,1)} %bitcast.44, bf16[128,640]{1,0:T(8,128)(2,1)S(1)} %maximum_maximum_fusion.lat_hbm, bf16[512,1024]{1,0:T(8,128)(2,1)S(1)} %copy-done.1, bf16[512,1024]{1,0:T(8,128)(2,1)S(1)} %copy-done.2), custom_call_target="tpu_custom_call" | custom-call | tf_op jit(solution)/shard_map/attention/pallas_call | solution.py:179
  82.2 0.0 copy-start
  82.2 1.3 copy-done
  83.5 0.0 copy-start.5
  83.5 115.4 %dispatch.1 = (bf16[5,2,4,4,72,256]{5,4,3,2,1,0:T(8,128)(2,1)}, bf16[5,256,256]{2,1,0:T(8,128)(2,1)}) custom-call(bf16[1024,1024]{1,0:T(8,128)(2,1)} %copy-done, bf16[1024,2560]{1,0:T(8,128)(2,1)} %wo_hbm.1, bf16[128,2560]{1,0:T(8,128)(2,1)} %bitcast.46, bf16[1152,1024]{1,0:T(8,128)(2,1)} %fusion.gm_ref), custom_call_target="tpu_custom_call" | custom-call | tf_op jit(solution)/shard_map/dispatch/pallas_call | solution.py:412
  198.9 0.0 copy-done.5
  198.9 0.6 broadcast_in_dim.42.gain_ref
  199.5 110.0 %experts.1 = bf16[128,2560]{1,0:T(8,128)(2,1)} custom-call(bf16[5,2,4,4,72,256]{5,4,3,2,1,0:T(8,128)(2,1)} %get-tuple-element.7.x_hbm, bf16[2560,768]{1,0:T(8,128)(2,1)} %bitcast.41, bf16[2560,768]{1,0:T(8,128)(2,1)} %bitcast.42, bf16[768,2560]{1,0:T(8,128)(2,1)} %bitcast.43, f32[1,2560]{1,0:T(1,128)} %broadcast_in_dim.42.gain_ref, ...), custom_call_target="tpu_custom_call" | custom-call | tf_op jit(solution)/shard_map/experts/pallas_call | solution.py:585
  309.5 2.0 copy.44
  (8 shorter events, 0.1 us)
Async XLA Ops:
  0.0 12.4 %copy-start.6 = (f32[1,128,6]{1,0,2:T(1,128)S(1)}, f32[1,128,6]{1,0,2:T(1,128)}, u32[]{:S(2)}) copy-start(f32[1,128,6]{1,0,2:T(1,128)} %param.22) | copy-start | bytes 9220
  20.7 4.3 %copy-start.4 = (bf16[1,128,64]{1,2,0:T(8,128)(2,1)S(1)}, bf16[1,128,64]{1,2,0:T(8,128)(2,1)}, u32[]{:S(2)}) copy-start(bf16[1,128,64]{1,2,0:T(8,128)(2,1)} %param.16) | copy-start | bytes 49156
  20.7 4.5 %copy-start.3 = (bf16[1,128,512]{2,1,0:T(8,128)(2,1)S(1)}, bf16[1,128,512]{2,1,0:T(8,128)(2,1)}, u32[]{:S(2)}) copy-start(bf16[1,128,512]{2,1,0:T(8,128)(2,1)} %param.15) | copy-start | bytes 393220
  20.7 4.6 %copy-start.1 = (bf16[512,1024]{1,0:T(8,128)(2,1)S(1)}, bf16[512,1024]{1,0:T(8,128)(2,1)}, u32[]{:S(2)}) copy-start(bf16[512,1024]{1,0:T(8,128)(2,1)} %uk_ref.1) | copy-start | bytes 3145732
  20.7 4.6 %copy-start.2 = (bf16[512,1024]{1,0:T(8,128)(2,1)S(1)}, bf16[512,1024]{1,0:T(8,128)(2,1)}, u32[]{:S(2)}) copy-start(bf16[512,1024]{1,0:T(8,128)(2,1)} %uv_ref.1) | copy-start | bytes 3145732
  82.2 1.3 copy-start
  83.5 115.4 %copy-start.5 = (f32[2560]{0:T(1024)S(1)}, f32[2560]{0:T(1024)}, u32[]{:S(2)}) copy-start(f32[2560]{0:T(1024)} %param.20) | copy-start | bytes 30724

commit v2 on v1

v2 whole, which is shorter than its diff:
```python
import functools
import math

import jax
import jax.numpy as jnp
from jax import lax
from jax.experimental import pallas as pl
from jax.experimental.pallas import tpu as pltpu
from jax.sharding import PartitionSpec as P

NOPE = 128
ROPE = 64
VDIM = 128
KVL = 512
D = 2560
FF = 768
TOPK = 6
CAP = 9
TOK = 128
LEN = 1024
QW = 1536
RING = 4
ROWS = 72
CHUNKS = 10
CW = 128
HALF = 1280
CHIP = 256
LATW = 640
MESH = pl.DeviceIdType.MESH
BF = jnp.bfloat16
F32 = jnp.float32
ANY = pl.BlockSpec(memory_space=pl.ANY)
VM = pl.BlockSpec(memory_space=pltpu.VMEM)
DMA = pltpu.SemaphoreType.DMA


def place():
    c = lax.axis_index("ctx")
    e = lax.axis_index("exp")
    return c // 2, c % 2, e // RING, e % RING


def device(y, core, z, x):
    return (y * 2 + core, z * RING + x)


def step(v, d):
    return lax.rem(v + d, RING)


def remote(src, dst, send, recv, target):
    return pltpu.make_async_remote_copy(
        src_ref=src, dst_ref=dst, send_sem=send, recv_sem=recv, device_id=target, device_id_type=MESH
    )


def greet(targets):
    barrier = pltpu.get_barrier_semaphore()
    for target in targets:
        pl.semaphore_signal(barrier, inc=1, device_id=target, device_id_type=MESH)
    pl.semaphore_wait(barrier, len(targets))


def attention_kernel(
    q_hbm, lat_hbm, uk_ref, uv_ref, out_ref, route_ref,
    qbuf, lat, kbuf, vbuf, q_send, q_recv, l_send, l_recv, own_sem,
):
    y, core, z, x = place()
    me = y * 2 + core
    peers = [(dy, dc) for dy in (0, 1, 3, 2) for dc in (0, 1) if (dy, dc) != (0, 0)]
    greet([device(step(y, dy), lax.rem(core + dc, 2), z, x) for dy, dc in peers])

    def lat_copy(dy):
        return remote(lat_hbm, lat.at[me], l_send.at[dy], l_recv.at[dy], device(step(y, dy), core, z, x))

    def lat_share(dy):
        block = lat.at[step(y, dy) * 2 + core]
        return remote(block, block, l_send.at[4 + dy], l_recv.at[4 + dy], device(y, 1 - core, z, x))

    def q_copy(dy, dc):
        i = dy * 2 + dc
        yy, cc = step(y, dy), lax.rem(core + dc, 2)
        columns = pl.ds(pl.multiple_of((yy * 2 + cc) * QW, 128), QW)
        return remote(q_hbm.at[:, columns], qbuf.at[me], q_send.at[i], q_recv.at[i], device(yy, cc, z, x))

    own_lat = pltpu.make_async_copy(lat_hbm, lat.at[me], own_sem.at[0])
    own_q = pltpu.make_async_copy(
        q_hbm.at[:, pl.ds(pl.multiple_of(me * QW, 128), QW)], qbuf.at[me], own_sem.at[1]
    )
    own_lat.start()
    own_q.start()
    for dy in (1, 3, 2):
        lat_copy(dy).start()
    for dy, dc in peers:
        q_copy(dy, dc).start()
    own_lat.wait()
    lat_share(0).start()
    for dy in (1, 3, 2):
        lat_copy(4 - dy).wait_recv()
        lat_share(dy).start()
    for dy in (0, 1, 3, 2):
        lat_share(dy).wait()
    for dy in (1, 3, 2):
        lat_copy(dy).wait_send()
    own_q.wait()

    lane = lax.broadcasted_iota(jnp.int32, (CHIP, 128), 1)

    def project(b, carry):
        rows = pl.ds(pl.multiple_of(b * CHIP, CHIP), CHIP)
        block = lat[pl.ds(b * 2, 2)].reshape(CHIP, LATW)
        latent = block[:, :KVL]
        route_ref[rows, :] = block[:, KVL:]
        rope = block[:, KVL:].astype(F32)
        rope_low = jnp.where(lane < 64, rope, 0.0).astype(BF)
        rope_high = pltpu.roll(rope, 64, 1)
        for h in range(8):
            nope = jnp.dot(latent, uk_ref[:, h * 128 : h * 128 + 128], preferred_element_type=F32)
            if h % 2 == 0:
                kbuf[h, rows, 0:128] = nope.astype(BF)
                kbuf[h, rows, 128:256] = rope_low
            else:
                turned = pltpu.roll(nope, 64, 1)
                kbuf[h, rows, 0:128] = jnp.where(lane < 64, 0.0, turned).astype(BF)
                kbuf[h, rows, 128:256] = jnp.where(lane < 64, turned, rope_high).astype(BF)
        vbuf[rows, :] = jnp.dot(latent, uv_ref[...], preferred_element_type=F32).astype(BF)
        return carry

    lax.fori_loop(0, RING, project, 0)

    factor = 1.0 / math.sqrt(NOPE + ROPE) * math.log2(math.e)
    row_at = lax.broadcasted_iota(jnp.int32, (CHIP, CHIP), 0)
    col_at = lax.broadcasted_iota(jnp.int32, (CHIP, CHIP), 1)
    causal = row_at >= col_at

    def attend(block):
        length = (block + 1) * CHIP

        def pair(p, carry):
            columns = pl.ds(pl.multiple_of(p * 384, 128), 384)
            q = qbuf[block * 2 : block * 2 + 2, :, columns].reshape(CHIP, 384)
            outs = []
            for odd in range(2):
                query = q[:, odd * 128 : odd * 128 + 256]
                head = p * 2 + odd
                contract = (((1,), (1,)), ((), ()))
                last = lax.dot_general(
                    query, kbuf[head, length - CHIP : length], contract, preferred_element_type=F32
                )
                last = jnp.where(causal, last, -jnp.inf)
                peak = jnp.max(last, axis=1, keepdims=True)
                if block:
                    first = lax.dot_general(
                        query, kbuf[head, 0 : length - CHIP], contract, preferred_element_type=F32
                    )
                    peak = jnp.maximum(peak, jnp.max(first, axis=1, keepdims=True))
                values = pl.ds(pl.multiple_of(head * 128, 128), 128)
                weight = jnp.exp2((last - peak) * factor)
                total = jnp.sum(weight, axis=1, keepdims=True)
                result = jnp.dot(
                    weight.astype(BF), vbuf[length - CHIP : length, values], preferred_element_type=F32
                )
                if block:
                    weight = jnp.exp2((first - peak) * factor)
                    total += jnp.sum(weight, axis=1, keepdims=True)
                    result += jnp.dot(
                        weight.astype(BF), vbuf[0 : length - CHIP, values], preferred_element_type=F32
                    )
                outs.append((result / total).astype(BF))
            out_ref[block * CHIP : (block + 1) * CHIP, pl.ds(pl.multiple_of(p * 256, 256), 256)] = (
                jnp.concatenate(outs, axis=1)
            )
            return carry

        lax.fori_loop(0, 4, pair, 0)

    for dy in (0, 1, 3, 2):
        for dc in range(2):
            if (dy, dc) != (0, 0):
                q_copy((4 - dy) % 4, dc).wait_recv()
        source = lax.rem(y + dy, RING)
        for block in range(RING):
            pl.when(source == block)(functools.partial(attend, block))
    for dy, dc in peers:
        q_copy(dy, dc).wait_send()


def attention_call(queries, latrope, w_uk, w_uv):
    return pl.pallas_call(
        attention_kernel,
        out_shape=(jax.ShapeDtypeStruct((LEN, 1024), BF), jax.ShapeDtypeStruct((LEN, 128), BF)),
        in_specs=[ANY, ANY, VM, VM],
        out_specs=(VM, VM),
        scratch_shapes=[
            pltpu.VMEM((8, TOK, QW), BF),
            pltpu.VMEM((8, TOK, LATW), BF),
            pltpu.VMEM((8, LEN, 256), BF),
            pltpu.VMEM((LEN, 1024), BF),
            DMA((8,)),
            DMA((8,)),
            DMA((8,)),
            DMA((8,)),
            DMA((2,)),
        ],
        compiler_params=pltpu.CompilerParams(
            collective_id=1, has_side_effects=True, vmem_limit_bytes=48 * 2**20
        ),
        name="attention",
    )(queries, latrope, w_uk, w_uv)


def exp_targets(y, core, z, x):
    found = [device(y, 1 - core, z, x)]
    for d in (1, 2, 3):
        found.append(device(step(y, d), core, z, x))
        found.append(device(y, core, step(z, d), x))
        found.append(device(y, core, z, step(x, d)))
    return found


def first_phase(j, spot, src, mid, send, recv, own):
    y, core, z, x = spot
    copies = []
    for d in (1, 3, 2):
        xx, zz = step(x, d), step(z, d)
        copies.append(
            remote(src.at[j, 0, :, xx], mid.at[j, 0, x], send.at[j, d], recv.at[j, d], device(y, core, z, xx))
        )
        copies.append(
            remote(
                src.at[j, 1, zz], mid.at[j, 1, z], send.at[j, 3 + d], recv.at[j, 3 + d], device(y, core, zz, x)
            )
        )
    copies.append(pltpu.make_async_copy(src.at[j, 0, :, x], mid.at[j, 0, x], own.at[j, 0]))
    copies.append(pltpu.make_async_copy(src.at[j, 1, z], mid.at[j, 1, z], own.at[j, 1]))
    return copies


def second_phase(j, spot, mid, dst, send, recv, own):
    y, core, z, x = spot
    copies = []
    for d in (1, 3, 2):
        xx, zz = step(x, d), step(z, d)
        copies.append(
            remote(mid.at[j, 0, :, zz], dst.at[j, 0, z], send.at[j, d], recv.at[j, d], device(y, core, zz, x))
        )
        copies.append(
            remote(
                mid.at[j, 1, :, xx],
                dst.at[j, 1, :, x],
                send.at[j, 3 + d],
                recv.at[j, 3 + d],
                device(y, core, z, xx),
            )
        )
    copies.append(pltpu.make_async_copy(mid.at[j, 0, :, z], dst.at[j, 0, z], own.at[j, 0]))
    copies.append(pltpu.make_async_copy(mid.at[j, 1, :, x], dst.at[j, 1, :, x], own.at[j, 1]))
    return copies


def pipeline(stages):
    def turn(t, carry):
        for lag, stage in reversed(stages):
            j = t - lag

            @pl.when((j >= 0) & (j < CHUNKS))
            def _(stage=stage, j=j):
                stage(j)

        return carry

    lax.fori_loop(0, CHUNKS + stages[-1][0], turn, 0)


def start_all(copies):
    for copy in copies:
        copy.start()


def wait_all(copies):
    for copy in copies:
        copy.wait()


def moe_kernel(
    mixed_hbm, wo_hbm, stream_hbm, route_ref, wg_hbm, wu_hbm, wd_hbm, gain_ref, out_ref,
    mixed, late, p_own, p_sib, r_core, rs_buf, hbuf, gs, t1, xbuf, pickers, wg, wu, wd, sx, hown, swap, spots,
    in_sem, wo_sem, w_sem, st_sem, c1_s, c1_r, rs_s, rs_r, ag_s, ag_r, c2_s, c2_r, p1_s, p1_r, p2_s, p2_r,
    d1_s, d1_r, d2_s, d2_r, c3_s, c3_r, fs_s, fs_r, sw_s, sw_r, o1, o2, o3, o4,
):
    spot = place()
    y, core, z, x = spot
    sibling = device(y, 1 - core, z, x)

    def columns(half, j):
        return pl.ds(pl.multiple_of(half * HALF + j * CW, 128), CW)

    def wo_copy(j, side):
        half = core if side == 0 else 1 - core
        return pltpu.make_async_copy(
            wo_hbm.at[:, :, :, columns(half, j)], late.at[j, side, :, :, 0:64], wo_sem.at[j, side]
        )

    def half_of(which):
        return pl.ds(pl.multiple_of(which * HALF, 128), HALF)

    mixed_copy = pltpu.make_async_copy(mixed_hbm, mixed.at[0:LEN], in_sem.at[0])
    stream_copy = pltpu.make_async_copy(stream_hbm.at[:, half_of(core)], sx.at[core], in_sem.at[1])
    weights = [
        pltpu.make_async_copy(wg_hbm, wg, w_sem.at[0]),
        pltpu.make_async_copy(wu_hbm, wu, w_sem.at[1]),
        pltpu.make_async_copy(wd_hbm, wd, w_sem.at[2]),
    ]
    mixed_copy.start()
    stream_copy.start()

    def load_wo(j, carry):
        for side in range(2):
            wo_copy(j, side).start()
        return carry

    lax.fori_loop(0, CHUNKS, load_wo, 0)
    start_all(weights)
    greet(exp_targets(y, core, z, x))
    stream_send = remote(
        stream_hbm.at[:, half_of(1 - core)], sx.at[core], st_sem.at[0], st_sem.at[1], sibling
    )
    stream_send.start()
    mixed_copy.wait()
    stream_copy.wait()

    def rows_of(which):
        return pl.ds(pl.multiple_of(which * CHIP, CHIP), CHIP)

    def core_sum(j, send, recv):
        return remote(p_sib.at[j], r_core.at[j], send.at[j], recv.at[j], sibling)

    def scatter(j, send, recv):
        return [
            remote(
                p_own.at[j, rows_of(step(y, d))],
                rs_buf.at[j, d - 1],
                send.at[j, d],
                recv.at[j, d],
                device(step(y, d), core, z, x),
            )
            for d in (1, 3, 2)
        ]

    def spread(j):
        block = hbuf.at[j, core, y, :, 0:64]
        return [
            remote(block, block, ag_s.at[j, d], ag_r.at[j, d], device(step(y, d), core, z, x))
            for d in (1, 3, 2)
        ]

    def core_share(j):
        block = hbuf.at[j, core, :, :, 0:64]
        return remote(block, block, c2_s.at[j], c2_r.at[j], sibling)

    def gather_row():
        row = lax.broadcasted_iota(jnp.int32, (1152, 128), 0)
        low = lax.broadcasted_iota(jnp.int32, (1152, 128), 1) * ROWS
        inside = (row >= low) & (row < low + ROWS)
        member = jnp.where(inside, 1.0, 0.0).astype(BF)
        at = jnp.sum(jnp.where(inside, row - low, 0).astype(F32), axis=1, keepdims=True)
        return member, at

    def route_spots():
        lane = lax.broadcasted_iota(jnp.int32, (TOK, 128), 1)
        first = ((y * 2 + core) * 16).astype(F32)
        wanted = jnp.where(lane < 16, lane.astype(F32) + first, -1.0)
        earlier = lax.broadcasted_iota(jnp.int32, (TOK, 128), 0) > lane
        earlier = jnp.where(earlier, 1.0, 0.0).astype(BF)
        for b in range(8):
            rows = slice(b * TOK, (b + 1) * TOK)
            route = route_ref[rows, :].astype(F32)
            named = jnp.zeros((TOK, 128), F32)
            gate = jnp.zeros((TOK, 128), F32)
            for k in range(TOPK):
                hit = route[:, 64 + k : 65 + k] == wanted
                named = jnp.where(hit, 1.0, named)
                gate = jnp.where(hit, route[:, 64 + TOPK + k : 65 + TOPK + k], gate)
            slot = jnp.dot(earlier, named.astype(BF), preferred_element_type=F32)
            spots[0, rows, :] = jnp.where(named > 0.0, slot + (b * CAP), -1.0).astype(BF)
            spots[1, rows, :] = gate.astype(BF)

    def pickers_in():
        member, at = gather_row()
        for b in range(RING):
            rows = slice(b * 288, (b + 1) * 288)
            wide = lax.dot_general(
                member[rows], spots[0], (((1,), (1,)), ((), ())), preferred_element_type=F32
            )
            pickers[rows, 0:LEN] = jnp.where(wide == at[rows], 1.0, 0.0).astype(BF)

    def pickers_out():
        low = lax.broadcasted_iota(jnp.int32, (128, 1152), 0) * ROWS
        row = lax.broadcasted_iota(jnp.int32, (128, 1152), 1)
        inside = (row >= low) & (row < low + ROWS)
        member = jnp.where(inside, 1.0, 0.0).astype(BF)
        at = jnp.sum(jnp.where(inside, row - low, 0).astype(F32), axis=0, keepdims=True)
        for b in range(RING):
            rows = slice(b * CHIP, (b + 1) * CHIP)
            wide = jnp.dot(spots[0, rows, :], member, preferred_element_type=F32)
            gate = jnp.dot(spots[1, rows, :], member, preferred_element_type=F32)
            pickers[rows, :] = jnp.where(wide == at, gate, 0.0).astype(BF)

    def one(j):
        return first_phase(j, spot, gs, t1, p1_s, p1_r, o1)

    def two(j):
        return second_phase(j, spot, t1, xbuf, p2_s, p2_r, o2)

    def project(j):
        for side in range(2):
            wo_copy(j, side).wait()
        own = late[j, 0, :, :, 0:64].reshape(1024, CW)
        other = late[j, 1, :, :, 0:64].reshape(1024, CW)
        both = jnp.concatenate([own, other], axis=1)

        def block(b, carry):
            rows = rows_of(b)
            product = jnp.dot(mixed[rows, :], both, preferred_element_type=F32).astype(BF)
            p_own[j, rows] = product[:, :CW]
            p_sib[j, rows] = product[:, CW:]
            return carry

        lax.fori_loop(0, RING, block, 0)
        core_sum(j, c1_s, c1_r).start()

    def add_core(j):
        core_sum(j, c1_s, c1_r).wait()
        p_own[j] = (p_own[j].astype(F32) + r_core[j].astype(F32)).astype(BF)
        start_all(scatter(j, rs_s, rs_r))

    def chip_total(j):
        total = p_own[j, rows_of(y)].astype(F32)
        for i in range(3):
            total += rs_buf[j, i].astype(F32)
        return total

    def finish_hidden(j):
        wait_all(scatter(j, rs_s, rs_r))
        stream = sx[:, :, pl.ds(pl.multiple_of(j * CW, 128), CW)].reshape(CHIP, CW)
        hidden = (stream.astype(F32) + chip_total(j)).astype(BF)
        hbuf[j, core, y, :, 0:64] = hidden.reshape(RING, 64, CW)
        hown[j] = hidden
        start_all(spread(j))

    def share(j):
        wait_all(spread(j))
        core_share(j).start()

    def pick(j):
        core_share(j).wait()
        both = jnp.concatenate(
            [hbuf[j, half, :, :, 0:64].reshape(1024, CW) for half in range(2)], axis=1
        )

        def block(b, carry):
            left = pickers[pl.ds(pl.multiple_of(b * 288, 16), 288), 0:LEN]
            picked = jnp.dot(left, both, preferred_element_type=F32).reshape(RING, ROWS, 2 * CW)
            gs[j, 0, b] = picked[:, :, :CW].astype(BF)
            gs[j, 1, b] = picked[:, :, CW:].astype(BF)
            return carry

        lax.fori_loop(0, RING, block, 0)
        start_all(one(j))

    def forward(j):
        wait_all(one(j))
        start_all(two(j))

    def drain(j):
        wait_all(two(j))

    def prepare(j):
        pl.when(j == 0)(route_spots)
        pl.when(j == 1)(pickers_in)

    stream_send.wait()
    pipeline(
        [
            (0, project),
            (1, add_core),
            (1, prepare),
            (3, finish_hidden),
            (5, share),
            (6, pick),
            (8, forward),
            (10, drain),
        ]
    )
    wait_all(weights)

    def hidden_units(b, carry):
        squares = jnp.zeros((288, 1), F32)
        for j in range(CHUNKS):
            for half in range(2):
                part = xbuf[j, half, b].astype(F32).reshape(288, CW)
                squares += jnp.sum(part * part, axis=1, keepdims=True)
        scale = lax.rsqrt(squares * (1.0 / D) + 1e-06)
        gate = jnp.zeros((288, FF), F32)
        up = jnp.zeros((288, FF), F32)
        for half in range(2):
            parts = []
            for j in range(CHUNKS):
                at = half * HALF + j * CW
                part = xbuf[j, half, b].astype(F32).reshape(288, CW)
                parts.append((part * scale * gain_ref[:, at : at + CW]).astype(BF))
            left = jnp.concatenate(parts, axis=1)
            gate += jnp.dot(left, wg[half * HALF : (half + 1) * HALF], preferred_element_type=F32)
            up += jnp.dot(left, wu[half * HALF : (half + 1) * HALF], preferred_element_type=F32)
        mixed[pl.ds(pl.multiple_of(b * 288, 16), 288), 0:FF] = (
            gate / (1.0 + jnp.exp(-gate)) * up
        ).astype(BF)
        return carry

    lax.fori_loop(0, RING, hidden_units, 0)

    def back_one(j):
        return first_phase(j, spot, gs, late, d1_s, d1_r, o3)

    def back_two(j):
        return second_phase(j, spot, late, hbuf, d2_s, d2_r, o4)

    def exchange(j):
        return remote(swap.at[j, 0], swap.at[j, 1], sw_s.at[j], sw_r.at[j], sibling)

    def down(j):
        both = jnp.concatenate([wd[:, columns(half, j)] for half in range(2)], axis=1)

        def block(b, carry):
            left = mixed[pl.ds(pl.multiple_of(b * 288, 16), 288), 0:FF]
            result = jnp.dot(left, both, preferred_element_type=F32).reshape(RING, ROWS, 2 * CW)
            gs[j, 0, b] = result[:, :, :CW].astype(BF)
            gs[j, 1, b] = result[:, :, CW:].astype(BF)
            return carry

        lax.fori_loop(0, RING, block, 0)
        start_all(back_one(j))

    def back_forward(j):
        wait_all(back_one(j))
        start_all(back_two(j))

    def combine(j):
        wait_all(back_two(j))
        both = jnp.concatenate(
            [
                hbuf[j, core].astype(F32).reshape(1152, CW).astype(BF),
                hbuf[j, 1 - core].astype(F32).reshape(1152, CW).astype(BF),
            ],
            axis=1,
        )

        def block(b, carry):
            rows = rows_of(b)
            product = jnp.dot(pickers[rows, :], both, preferred_element_type=F32).astype(BF)
            p_own[j, rows] = product[:, :CW]
            p_sib[j, rows] = product[:, CW:]
            return carry

        lax.fori_loop(0, RING, block, 0)
        core_sum(j, c3_s, c3_r).start()

    def add_back(j):
        core_sum(j, c3_s, c3_r).wait()
        p_own[j] = (p_own[j].astype(F32) + r_core[j].astype(F32)).astype(BF)
        start_all(scatter(j, fs_s, fs_r))

    def finish(j):
        wait_all(scatter(j, fs_s, fs_r))
        total = (hown[j].astype(F32) + chip_total(j)).astype(BF)
        swap[j, 0] = jnp.where(core == 0, total[TOK:], total[:TOK])
        exchange(j).start()
        out_ref[:, columns(core, j)] = jnp.where(core == 0, total[:TOK], total[TOK:])

    def land(j):
        exchange(j).wait()
        out_ref[:, columns(1 - core, j)] = swap[j, 1]

    def prepare_back(j):
        pl.when(j == 0)(pickers_out)

    pipeline(
        [
            (0, down),
            (1, prepare_back),
            (2, back_forward),
            (4, combine),
            (5, add_back),
            (7, finish),
            (8, land),
        ]
    )


def moe_call(mixed, w_o, stream, route, w_gate, w_up, w_down, gain):
    grid_rows = (CHUNKS, 2, RING, RING, ROWS, CW)
    one = DMA((CHUNKS,))
    ring = DMA((CHUNKS, 4))
    phase = DMA((CHUNKS, 7))
    return pl.pallas_call(
        moe_kernel,
        out_shape=jax.ShapeDtypeStruct((TOK, D), BF),
        in_specs=[ANY, ANY, ANY, VM, ANY, ANY, ANY, VM],
        out_specs=VM,
        scratch_shapes=[
            pltpu.VMEM((1152, 1024), BF),
            pltpu.VMEM(grid_rows, BF),
            pltpu.VMEM((CHUNKS, LEN, CW), BF),
            pltpu.VMEM((CHUNKS, LEN, CW), BF),
            pltpu.VMEM((CHUNKS, LEN, CW), BF),
            pltpu.VMEM((CHUNKS, 3, CHIP, CW), BF),
            pltpu.VMEM(grid_rows, BF),
            pltpu.VMEM(grid_rows, BF),
            pltpu.VMEM(grid_rows, BF),
            pltpu.VMEM(grid_rows, BF),
            pltpu.VMEM((1152, 1152), BF),
            pltpu.VMEM((D, FF), BF),
            pltpu.VMEM((D, FF), BF),
            pltpu.VMEM((FF, D), BF),
            pltpu.VMEM((2, TOK, HALF), BF),
            pltpu.VMEM((CHUNKS, CHIP, CW), BF),
            pltpu.VMEM((CHUNKS, 2, TOK, CW), BF),
            pltpu.VMEM((2, LEN, 128), BF),
            DMA((2,)),
            DMA((CHUNKS, 2)),
            DMA((3,)),
            DMA((2,)),
            *[one, one, ring, ring, ring, ring, one, one],
            *[phase] * 8,
            *[one, one, ring, ring, one, one],
            *[DMA((CHUNKS, 2))] * 4,
        ],
        compiler_params=pltpu.CompilerParams(
            collective_id=2, has_side_effects=True, vmem_limit_bytes=63 * 2**20
        ),
        name="moe",
    )(mixed, w_o, stream, route, w_gate, w_up, w_down, gain)


def local(
    stream_in,
    queries,
    latents,
    key_rope,
    w_uk,
    w_uv,
    w_o,
    norm_gain,
    expert_ids,
    gate_weights,
    w_gate,
    w_up,
    w_down,
):
    packed = jnp.concatenate(
        [latents[0], key_rope[0], expert_ids[0].astype(BF), gate_weights[0].astype(BF), jnp.zeros((TOK, 52), BF)],
        axis=1,
    )
    mixed, route = attention_call(queries[0], packed, w_uk, w_uv)
    blocks = w_o.reshape(RING, RING, 64, D)
    out = moe_call(
        mixed, blocks, stream_in[0], route, w_gate[0], w_up[0], w_down[0], norm_gain[None, :]
    )
    return out[None]


def solution(mesh):
    return jax.shard_map(
        local,
        mesh=mesh,
        in_specs=(
            P("exp", "ctx", None),
            P("exp", "ctx", None),
            P("exp", "ctx", None),
            P("exp", "ctx", None),
            P(None, "ctx"),
            P(None, "ctx"),
            P("ctx", None),
            P(),
            P("exp", "ctx", None),
            P("exp", "ctx", None),
            P(("ctx", "exp"), None, None),
            P(("ctx", "exp"), None, None),
            P(("ctx", "exp"), None, None),
        ),
        out_specs=P("exp", "ctx", None),
        check_vma=False,
    )
```

time: 315 us -> 259 us (0.82)
  Pallas kernels: 282 us -> 245 us
  blocking collectives: 19.4 us -> 0 us
  local copies, waits for them, and re-layouts: 4.22 us -> 11.2 us
  matrix products: 3.17 us -> 0 us
    pallas_call x3 -> x2, Pallas kernels: 282 us -> 245 us  [the longest x1 194 us: moe_call(): pl.pallas_call(moe_kernel, out_shape=jax.ShapeDtypeStruct((TOK, D), BF),...]
    all_gather x2 -> x0, blocking collectives: 19.4 us -> none  [the longest x1 11.2 us: routing(): ids = lax.all_gather(expert_ids, 'ctx', axis=0, tiled=True)]
    unnamed x18 -> x12, local copies, waits for them, and re-layouts: 3.44 us -> 8.86 us
    dot_general x3 -> x0, matrix products: 3.17 us -> none  [the longest x1 2.24 us: routing(): gate_wide = jnp.dot(gate.astype(BF), widen, preferred_element_type=F32)]
where the time goes in v2:
time: 259 us; the launch traced here: 256 us
  Pallas kernels  245 us (95%)
  local copies, waits for them, and re-layouts  11.2 us (4%)
    pallas_call x1, Pallas kernels, moe_call(): pl.pallas_call(moe_kernel, out_shape=jax.ShapeDtypeStruct((TOK, D), BF),...  194 us
    pallas_call x1, Pallas kernels, attention_call(): pl.pallas_call(attention_kernel, out_shape=(jax.ShapeDtypeStruct((LEN, 10...  50.4 us
    unnamed x12, local copies, waits for them, and re-layouts  8.86 us

profile of v2, /device:TPU:34, one launch (start us, length us, event | category | flops | bytes accessed | tf_op | source)
XLA Modules:
  0.0 256.0 jit_solution(16765051948732246033)
XLA Ops:
  0.0 1.3 broadcast_in_dim.10.gain_ref
  1.3 0.8 copy.14
  2.1 0.8 copy.16
  2.9 0.8 copy.15
  3.8 1.0 concatenate.3.lat_hbm
  4.8 0.0 copy-start.1
  4.8 1.2 copy-done.1
  6.0 0.0 copy-start.2
  6.0 1.2 copy-done.2
  7.2 50.4 %attention.1 = (bf16[1024,1024]{1,0:T(8,128)(2,1)S(1)}, bf16[1024,128]{1,0:T(8,128)(2,1)S(1)}) custom-call(bf16[128,12288]{1,0:T(8,128)(2,1)} %bitcast.18, bf16[128,640]{1,0:T(8,128)(2,1)S(1)} %concatenate.3.lat_hbm, bf16[512,1024]{1,0:T(8,128)(2,1)S(1)} %copy-done.1, bf16[512,1024]{1,0:T(8,128)(2,1)S(1)} %copy-done.2), custom_call_target="tpu_custom_call" | custom-call | tf_op jit(solution)/shard_map/attention/pallas_call | solution.py:189
  57.6 0.0 copy-start
  57.6 1.3 copy-done
  58.9 0.0 copy-start.3
  58.9 0.7 copy-done.3
  59.6 194.4 %moe.1 = bf16[128,2560]{1,0:T(8,128)(2,1)} custom-call(bf16[1024,1024]{1,0:T(8,128)(2,1)} %copy-done, bf16[4,4,64,2560]{3,2,1,0:T(8,128)(2,1)} %bitcast.14, bf16[128,2560]{1,0:T(8,128)(2,1)} %bitcast.20, bf16[1024,128]{1,0:T(8,128)(2,1)} %copy-done.3, bf16[2560,768]{1,0:T(8,128)(2,1)} %bitcast.15, bf16[2560,768]{1,0:T(8,128)(2,1)} %bitcast.16, ...), custom_call_target="tpu_custom_call" | custom-call | tf_op jit(solution)/shard_map/moe/pallas_call | solution.py:605
  254.1 2.0 copy.18
  (2 shorter events, 0.0 us)
Async XLA Ops:
  4.8 1.2 copy-start.1
  6.0 1.2 copy-start.2
  57.6 1.3 copy-start
  58.9 0.7 copy-start.3

commit v3 on v2

--- a/solution.py
+++ b/solution.py
@@ -23,6 +23,7 @@
 ROWS = 72
 CHUNKS = 10
 CW = 128
+SLOTS = 4
 HALF = 1280
 CHIP = 256
 LATW = 640
@@ -220,19 +221,20 @@
 
 def first_phase(j, spot, src, mid, send, recv, own):
     y, core, z, x = spot
+    cut = lax.rem(j, SLOTS)
     copies = []
     for d in (1, 3, 2):
         xx, zz = step(x, d), step(z, d)
         copies.append(
-            remote(src.at[j, 0, :, xx], mid.at[j, 0, x], send.at[j, d], recv.at[j, d], device(y, core, z, xx))
+            remote(src.at[cut, 0, :, xx], mid.at[j, 0, x], send.at[j, d], recv.at[j, d], device(y, core, z, xx))
         )
         copies.append(
             remote(
-                src.at[j, 1, zz], mid.at[j, 1, z], send.at[j, 3 + d], recv.at[j, 3 + d], device(y, core, zz, x)
+                src.at[cut, 1, zz], mid.at[j, 1, z], send.at[j, 3 + d], recv.at[j, 3 + d], device(y, core, zz, x)
             )
         )
-    copies.append(pltpu.make_async_copy(src.at[j, 0, :, x], mid.at[j, 0, x], own.at[j, 0]))
-    copies.append(pltpu.make_async_copy(src.at[j, 1, z], mid.at[j, 1, z], own.at[j, 1]))
+    copies.append(pltpu.make_async_copy(src.at[cut, 0, :, x], mid.at[j, 0, x], own.at[j, 0]))
+    copies.append(pltpu.make_async_copy(src.at[cut, 1, z], mid.at[j, 1, z], own.at[j, 1]))
     return copies
 
 
@@ -284,7 +286,7 @@
 
 def moe_kernel(
     mixed_hbm, wo_hbm, stream_hbm, route_ref, wg_hbm, wu_hbm, wd_hbm, gain_ref, out_ref,
-    mixed, late, p_own, p_sib, r_core, rs_buf, hbuf, gs, t1, xbuf, pickers, wg, wu, wd, sx, hown, swap, spots,
+    mixed, late, p_own, p_sib, r_core, rs_buf, hbuf, gs, t1, xbuf, pickers, wg, wu, wd, sx, hown, swap, spots, units, squares,
     in_sem, wo_sem, w_sem, st_sem, c1_s, c1_r, rs_s, rs_r, ag_s, ag_r, c2_s, c2_r, p1_s, p1_r, p2_s, p2_r,
     d1_s, d1_r, d2_s, d2_r, c3_s, c3_r, fs_s, fs_r, sw_s, sw_r, o1, o2, o3, o4,
 ):
@@ -333,13 +335,14 @@
         return pl.ds(pl.multiple_of(which * CHIP, CHIP), CHIP)
 
     def core_sum(j, send, recv):
-        return remote(p_sib.at[j], r_core.at[j], send.at[j], recv.at[j], sibling)
+        slot = lax.rem(j, 2)
+        return remote(p_sib.at[slot], r_core.at[slot], send.at[j], recv.at[j], sibling)
 
     def scatter(j, send, recv):
         return [
             remote(
-                p_own.at[j, rows_of(step(y, d))],
-                rs_buf.at[j, d - 1],
+                p_own.at[lax.rem(j, SLOTS), rows_of(step(y, d))],
+                rs_buf.at[lax.rem(j, SLOTS), d - 1],
                 send.at[j, d],
                 recv.at[j, d],
                 device(step(y, d), core, z, x),
@@ -422,8 +425,8 @@
         def block(b, carry):
             rows = rows_of(b)
             product = jnp.dot(mixed[rows, :], both, preferred_element_type=F32).astype(BF)
-            p_own[j, rows] = product[:, :CW]
-            p_sib[j, rows] = product[:, CW:]
+            p_own[lax.rem(j, SLOTS), rows] = product[:, :CW]
+            p_sib[lax.rem(j, 2), rows] = product[:, CW:]
             return carry
 
         lax.fori_loop(0, RING, block, 0)
@@ -431,13 +434,15 @@
 
     def add_core(j):
         core_sum(j, c1_s, c1_r).wait()
-        p_own[j] = (p_own[j].astype(F32) + r_core[j].astype(F32)).astype(BF)
+        slot = lax.rem(j, SLOTS)
+        p_own[slot] = (p_own[slot].astype(F32) + r_core[lax.rem(j, 2)].astype(F32)).astype(BF)
         start_all(scatter(j, rs_s, rs_r))
 
     def chip_total(j):
-        total = p_own[j, rows_of(y)].astype(F32)
+        slot = lax.rem(j, SLOTS)
+        total = p_own[slot, rows_of(y)].astype(F32)
         for i in range(3):
-            total += rs_buf[j, i].astype(F32)
+            total += rs_buf[slot, i].astype(F32)
         return total
 
     def finish_hidden(j):
@@ -461,8 +466,8 @@
         def block(b, carry):
             left = pickers[pl.ds(pl.multiple_of(b * 288, 16), 288), 0:LEN]
             picked = jnp.dot(left, both, preferred_element_type=F32).reshape(RING, ROWS, 2 * CW)
-            gs[j, 0, b] = picked[:, :, :CW].astype(BF)
-            gs[j, 1, b] = picked[:, :, CW:].astype(BF)
+            gs[lax.rem(j, SLOTS), 0, b] = picked[:, :, :CW].astype(BF)
+            gs[lax.rem(j, SLOTS), 1, b] = picked[:, :, CW:].astype(BF)
             return carry
 
         lax.fori_loop(0, RING, block, 0)
@@ -475,9 +480,34 @@
     def drain(j):
         wait_all(two(j))
 
+        @pl.when(j == 0)
+        def _():
+            wait_all(weights)
+
+        gains = [gain_ref[pl.ds(half * CHUNKS + j, 1), :] for half in range(2)]
+        firsts = [pl.ds(pl.multiple_of(half * HALF + j * CW, 128), CW) for half in range(2)]
+        right_gate = jnp.concatenate([wg[rows, :] for rows in firsts], axis=0)
+        right_up = jnp.concatenate([wu[rows, :] for rows in firsts], axis=0)
+
+        def block(b, carry):
+            rows = pl.ds(pl.multiple_of(b * 288, 16), 288)
+            parts = [xbuf[j, half, b].astype(F32).reshape(288, CW) for half in range(2)]
+            squares[rows, :] += parts[0] * parts[0] + parts[1] * parts[1]
+            left = jnp.concatenate([(p * g).astype(BF) for p, g in zip(parts, gains)], axis=1)
+            units[rows, 0:FF] += jnp.dot(left, right_gate, preferred_element_type=F32)
+            units[rows, FF : 2 * FF] += jnp.dot(left, right_up, preferred_element_type=F32)
+            return carry
+
+        lax.fori_loop(0, RING, block, 0)
+
+    def clear():
+        units[...] = jnp.zeros((1152, 2 * FF), F32)
+        squares[...] = jnp.zeros((1152, CW), F32)
+
     def prepare(j):
         pl.when(j == 0)(route_spots)
         pl.when(j == 1)(pickers_in)
+        pl.when(j == 2)(clear)
 
     stream_send.wait()
     pipeline(
@@ -492,32 +522,17 @@
             (10, drain),
         ]
     )
-    wait_all(weights)
 
     def hidden_units(b, carry):
-        squares = jnp.zeros((288, 1), F32)
-        for j in range(CHUNKS):
-            for half in range(2):
-                part = xbuf[j, half, b].astype(F32).reshape(288, CW)
-                squares += jnp.sum(part * part, axis=1, keepdims=True)
-        scale = lax.rsqrt(squares * (1.0 / D) + 1e-06)
-        gate = jnp.zeros((288, FF), F32)
-        up = jnp.zeros((288, FF), F32)
-        for half in range(2):
-            parts = []
-            for j in range(CHUNKS):
-                at = half * HALF + j * CW
-                part = xbuf[j, half, b].astype(F32).reshape(288, CW)
-                parts.append((part * scale * gain_ref[:, at : at + CW]).astype(BF))
-            left = jnp.concatenate(parts, axis=1)
-            gate += jnp.dot(left, wg[half * HALF : (half + 1) * HALF], preferred_element_type=F32)
-            up += jnp.dot(left, wu[half * HALF : (half + 1) * HALF], preferred_element_type=F32)
-        mixed[pl.ds(pl.multiple_of(b * 288, 16), 288), 0:FF] = (
-            gate / (1.0 + jnp.exp(-gate)) * up
-        ).astype(BF)
+        rows = pl.ds(pl.multiple_of(b * 144, 16), 144)
+        total = jnp.sum(squares[rows, :], axis=1, keepdims=True)
+        scale = lax.rsqrt(total * (1.0 / D) + 1e-06)
+        gate = units[rows, 0:FF] * scale
+        up = units[rows, FF : 2 * FF] * scale
+        mixed[rows, 0:FF] = (gate / (1.0 + jnp.exp(-gate)) * up).astype(BF)
         return carry
 
-    lax.fori_loop(0, RING, hidden_units, 0)
+    lax.fori_loop(0, 8, hidden_units, 0)
 
     def back_one(j):
         return first_phase(j, spot, gs, late, d1_s, d1_r, o3)
@@ -526,7 +541,8 @@
         return second_phase(j, spot, late, hbuf, d2_s, d2_r, o4)
 
     def exchange(j):
-        return remote(swap.at[j, 0], swap.at[j, 1], sw_s.at[j], sw_r.at[j], sibling)
+        slot = lax.rem(j, 2)
+        return remote(swap.at[slot, 0], swap.at[slot, 1], sw_s.at[j], sw_r.at[j], sibling)
 
     def down(j):
         both = jnp.concatenate([wd[:, columns(half, j)] for half in range(2)], axis=1)
@@ -534,8 +550,8 @@
         def block(b, carry):
             left = mixed[pl.ds(pl.multiple_of(b * 288, 16), 288), 0:FF]
             result = jnp.dot(left, both, preferred_element_type=F32).reshape(RING, ROWS, 2 * CW)
-            gs[j, 0, b] = result[:, :, :CW].astype(BF)
-            gs[j, 1, b] = result[:, :, CW:].astype(BF)
+            gs[lax.rem(j, SLOTS), 0, b] = result[:, :, :CW].astype(BF)
+            gs[lax.rem(j, SLOTS), 1, b] = result[:, :, CW:].astype(BF)
             return carry
 
         lax.fori_loop(0, RING, block, 0)
@@ -558,8 +574,8 @@
         def block(b, carry):
             rows = rows_of(b)
             product = jnp.dot(pickers[rows, :], both, preferred_element_type=F32).astype(BF)
-            p_own[j, rows] = product[:, :CW]
-            p_sib[j, rows] = product[:, CW:]
+            p_own[lax.rem(j, SLOTS), rows] = product[:, :CW]
+            p_sib[lax.rem(j, 2), rows] = product[:, CW:]
             return carry
 
         lax.fori_loop(0, RING, block, 0)
@@ -567,19 +583,20 @@
 
     def add_back(j):
         core_sum(j, c3_s, c3_r).wait()
-        p_own[j] = (p_own[j].astype(F32) + r_core[j].astype(F32)).astype(BF)
+        slot = lax.rem(j, SLOTS)
+        p_own[slot] = (p_own[slot].astype(F32) + r_core[lax.rem(j, 2)].astype(F32)).astype(BF)
         start_all(scatter(j, fs_s, fs_r))
 
     def finish(j):
         wait_all(scatter(j, fs_s, fs_r))
         total = (hown[j].astype(F32) + chip_total(j)).astype(BF)
-        swap[j, 0] = jnp.where(core == 0, total[TOK:], total[:TOK])
+        swap[lax.rem(j, 2), 0] = jnp.where(core == 0, total[TOK:], total[:TOK])
         exchange(j).start()
         out_ref[:, columns(core, j)] = jnp.where(core == 0, total[:TOK], total[TOK:])
 
     def land(j):
         exchange(j).wait()
-        out_ref[:, columns(1 - core, j)] = swap[j, 1]
+        out_ref[:, columns(1 - core, j)] = swap[lax.rem(j, 2), 1]
 
     def prepare_back(j):
         pl.when(j == 0)(pickers_out)
@@ -610,12 +627,12 @@
         scratch_shapes=[
             pltpu.VMEM((1152, 1024), BF),
             pltpu.VMEM(grid_rows, BF),
-            pltpu.VMEM((CHUNKS, LEN, CW), BF),
-            pltpu.VMEM((CHUNKS, LEN, CW), BF),
-            pltpu.VMEM((CHUNKS, LEN, CW), BF),
-            pltpu.VMEM((CHUNKS, 3, CHIP, CW), BF),
+            pltpu.VMEM((SLOTS, LEN, CW), BF),
+            pltpu.VMEM((2, LEN, CW), BF),
+            pltpu.VMEM((2, LEN, CW), BF),
+            pltpu.VMEM((SLOTS, 3, CHIP, CW), BF),
             pltpu.VMEM(grid_rows, BF),
-            pltpu.VMEM(grid_rows, BF),
+            pltpu.VMEM((SLOTS, *grid_rows[1:]), BF),
             pltpu.VMEM(grid_rows, BF),
             pltpu.VMEM(grid_rows, BF),
             pltpu.VMEM((1152, 1152), BF),
@@ -624,8 +641,10 @@
             pltpu.VMEM((FF, D), BF),
             pltpu.VMEM((2, TOK, HALF), BF),
             pltpu.VMEM((CHUNKS, CHIP, CW), BF),
-            pltpu.VMEM((CHUNKS, 2, TOK, CW), BF),
+            pltpu.VMEM((2, 2, TOK, CW), BF),
             pltpu.VMEM((2, LEN, 128), BF),
+            pltpu.VMEM((1152, 2 * FF), F32),
+            pltpu.VMEM((1152, CW), F32),
             DMA((2,)),
             DMA((CHUNKS, 2)),
             DMA((3,)),
@@ -664,7 +683,7 @@
     mixed, route = attention_call(queries[0], packed, w_uk, w_uv)
     blocks = w_o.reshape(RING, RING, 64, D)
     out = moe_call(
-        mixed, blocks, stream_in[0], route, w_gate[0], w_up[0], w_down[0], norm_gain[None, :]
+        mixed, blocks, stream_in[0], route, w_gate[0], w_up[0], w_down[0], norm_gain.reshape(2 * CHUNKS, CW)
     )
     return out[None]
 

time: 259 us -> 249 us (0.961)
  Pallas kernels: 245 us -> 237 us
    pallas_call x1, Pallas kernels: 194 us -> 186 us  [moe_call(): pl.pallas_call(moe_kernel, out_shape=jax.ShapeDtypeStruct((TOK, D), BF),...]
where the time goes in v3:
time: 249 us; the launch traced here: 247 us
  Pallas kernels  237 us (95%)
  local copies, waits for them, and re-layouts  9.89 us (4%)
    pallas_call x1, Pallas kernels, moe_call(): pl.pallas_call(moe_kernel, out_shape=jax.ShapeDtypeStruct((TOK, D), BF),...  186 us
    pallas_call x1, Pallas kernels, attention_call(): pl.pallas_call(attention_kernel, out_shape=(jax.ShapeDtypeStruct((LEN, 10...  50.4 us
    unnamed x12, local copies, waits for them, and re-layouts  8.86 us

profile of v3, /device:TPU:34, one launch (start us, length us, event | category | flops | bytes accessed | tf_op | source)
XLA Modules:
  0.0 246.7 jit_solution(8178330603702722266)
XLA Ops:
  0.0 0.8 copy.14
  0.8 0.8 copy.16
  1.6 0.8 copy.15
  2.5 1.0 concatenate.3.lat_hbm
  3.5 0.0 copy-start.1
  3.5 1.2 copy-done.1
  4.7 0.0 copy-start.2
  4.7 1.2 copy-done.2
  5.9 50.4 %attention.1 = (bf16[1024,1024]{1,0:T(8,128)(2,1)S(1)}, bf16[1024,128]{1,0:T(8,128)(2,1)S(1)}) custom-call(bf16[128,12288]{1,0:T(8,128)(2,1)} %bitcast.19, bf16[128,640]{1,0:T(8,128)(2,1)S(1)} %concatenate.3.lat_hbm, bf16[512,1024]{1,0:T(8,128)(2,1)S(1)} %copy-done.1, bf16[512,1024]{1,0:T(8,128)(2,1)S(1)} %copy-done.2), custom_call_target="tpu_custom_call" | custom-call | tf_op jit(solution)/shard_map/attention/pallas_call | solution.py:190
  56.3 0.0 copy-start
  56.3 1.3 copy-done
  57.6 0.0 copy-start.3
  57.6 0.7 copy-done.3
  58.3 186.4 %moe.1 = bf16[128,2560]{1,0:T(8,128)(2,1)} custom-call(bf16[1024,1024]{1,0:T(8,128)(2,1)} %copy-done, bf16[4,4,64,2560]{3,2,1,0:T(8,128)(2,1)} %bitcast.15, bf16[128,2560]{1,0:T(8,128)(2,1)} %bitcast.21, bf16[1024,128]{1,0:T(8,128)(2,1)} %copy-done.3, bf16[2560,768]{1,0:T(8,128)(2,1)} %bitcast.16, bf16[2560,768]{1,0:T(8,128)(2,1)} %bitcast.17, ...), custom_call_target="tpu_custom_call" | custom-call | tf_op jit(solution)/shard_map/moe/pallas_call | solution.py:622
  244.7 2.0 copy.18
  (2 shorter events, 0.0 us)
Async XLA Ops:
  3.5 1.2 copy-start.1
  4.7 1.2 copy-start.2
  56.3 1.3 copy-start
  57.6 0.7 copy-start.3

commit v4 on v3

v4 whole, which is shorter than its diff:
```python
import functools
import math

import jax
import jax.numpy as jnp
from jax import lax
from jax.experimental import pallas as pl
from jax.experimental.pallas import tpu as pltpu
from jax.sharding import PartitionSpec as P

NOPE = 128
ROPE = 64
VDIM = 128
KVL = 512
D = 2560
FF = 768
TOPK = 6
CAP = 9
TOK = 128
LEN = 1024
QW = 1536
RING = 4
ROWS = 72
CHUNKS = 10
CW = 128
SLOTS = 4
ROWS_IN = 5
HALF = 1280
CHIP = 256
LATW = 640
MESH = pl.DeviceIdType.MESH
BF = jnp.bfloat16
F32 = jnp.float32
ANY = pl.BlockSpec(memory_space=pl.ANY)
VM = pl.BlockSpec(memory_space=pltpu.VMEM)
DMA = pltpu.SemaphoreType.DMA


def place():
    c = lax.axis_index("ctx")
    e = lax.axis_index("exp")
    return c // 2, c % 2, e // RING, e % RING


def device(y, core, z, x):
    return (y * 2 + core, z * RING + x)


def step(v, d):
    return lax.rem(v + d, RING)


def remote(src, dst, send, recv, target):
    return pltpu.make_async_remote_copy(
        src_ref=src, dst_ref=dst, send_sem=send, recv_sem=recv, device_id=target, device_id_type=MESH
    )


def greet(targets):
    barrier = pltpu.get_barrier_semaphore()
    for target in targets:
        pl.semaphore_signal(barrier, inc=1, device_id=target, device_id_type=MESH)
    pl.semaphore_wait(barrier, len(targets))


def exp_targets(y, core, z, x):
    found = [device(y, 1 - core, z, x)]
    for d in (1, 2, 3):
        found.append(device(step(y, d), core, z, x))
        found.append(device(y, core, step(z, d), x))
        found.append(device(y, core, z, step(x, d)))
    return found


def first_phase(j, spot, src, mid, send, recv, own):
    y, core, z, x = spot
    cut = lax.rem(j, SLOTS)
    copies = []
    for d in (1, 3, 2):
        xx, zz = step(x, d), step(z, d)
        copies.append(
            remote(src.at[cut, 0, :, xx], mid.at[j, 0, x], send.at[j, d], recv.at[j, d], device(y, core, z, xx))
        )
        copies.append(
            remote(
                src.at[cut, 1, zz], mid.at[j, 1, z], send.at[j, 3 + d], recv.at[j, 3 + d], device(y, core, zz, x)
            )
        )
    copies.append(pltpu.make_async_copy(src.at[cut, 0, :, x], mid.at[j, 0, x], own.at[j, 0]))
    copies.append(pltpu.make_async_copy(src.at[cut, 1, z], mid.at[j, 1, z], own.at[j, 1]))
    return copies


def second_phase(j, spot, mid, dst, cut, send, recv, own):
    y, core, z, x = spot
    copies = []
    for d in (1, 3, 2):
        xx, zz = step(x, d), step(z, d)
        copies.append(
            remote(mid.at[j, 0, :, zz], dst.at[cut, 0, z], send.at[j, d], recv.at[j, d], device(y, core, zz, x))
        )
        copies.append(
            remote(
                mid.at[j, 1, :, xx],
                dst.at[cut, 1, :, x],
                send.at[j, 3 + d],
                recv.at[j, 3 + d],
                device(y, core, z, xx),
            )
        )
    copies.append(pltpu.make_async_copy(mid.at[j, 0, :, z], dst.at[cut, 0, z], own.at[j, 0]))
    copies.append(pltpu.make_async_copy(mid.at[j, 1, :, x], dst.at[cut, 1, :, x], own.at[j, 1]))
    return copies


def pipeline(stages):
    def turn(t, carry):
        for lag, stage in reversed(stages):
            j = t - lag

            @pl.when((j >= 0) & (j < CHUNKS))
            def _(stage=stage, j=j):
                stage(j)

        return carry

    lax.fori_loop(0, CHUNKS + stages[-1][0], turn, 0)


def start_all(copies):
    for copy in copies:
        copy.start()


def wait_all(copies):
    for copy in copies:
        copy.wait()


def moe_kernel(
    q_hbm, lat_hbm, uk_hbm, uv_hbm, wo_hbm, stream_hbm, wg_hbm, wu_hbm, wd_hbm, gain_ref, out_ref,
    qbuf, lat, q_send, q_recv, l_send, l_recv, own_sem,
    mixed, late, p_own, p_sib, r_core, rs_buf, hbuf, gs, t1, xbuf, pickers, wg, wu, wd, sx, hown, swap, spots,
    in_sem, wo_sem, w_sem, st_sem, c1_s, c1_r, rs_s, rs_r, ag_s, ag_r, c2_s, c2_r, p1_s, p1_r, p2_s, p2_r,
    d1_s, d1_r, d2_s, d2_r, c3_s, c3_r, fs_s, fs_r, sw_s, sw_r, o1, o2, o3, o4,
):
    spot = place()
    y, core, z, x = spot
    sibling = device(y, 1 - core, z, x)

    def columns(half, j):
        return pl.ds(pl.multiple_of(half * HALF + j * CW, 128), CW)

    def wo_copy(j, side):
        half = core if side == 0 else 1 - core
        return pltpu.make_async_copy(
            wo_hbm.at[:, :, :, columns(half, j)], late.at[j, side, :, :, 0:64], wo_sem.at[j, side]
        )

    def half_of(which):
        return pl.ds(pl.multiple_of(which * HALF, 128), HALF)

    stream_copy = pltpu.make_async_copy(stream_hbm.at[:, half_of(core)], sx.at[core], in_sem.at[1])
    weights = [
        pltpu.make_async_copy(wg_hbm, wg, w_sem.at[0]),
        pltpu.make_async_copy(wu_hbm, wu, w_sem.at[1]),
        pltpu.make_async_copy(wd_hbm, wd, w_sem.at[2]),
    ]
    me = y * 2 + core

    def lat_copy(dy):
        return remote(lat_hbm, lat.at[me], l_send.at[dy], l_recv.at[dy], device(step(y, dy), core, z, x))

    def lat_share(dy):
        block = lat.at[step(y, dy) * 2 + core]
        return remote(block, block, l_send.at[4 + dy], l_recv.at[4 + dy], device(y, 1 - core, z, x))

    def q_copy(dy, dc):
        i = dy * 2 + dc
        yy, cc = step(y, dy), lax.rem(core + dc, 2)
        columns = pl.ds(pl.multiple_of((yy * 2 + cc) * QW, 128), QW)
        return remote(q_hbm.at[:, columns], qbuf.at[me], q_send.at[i], q_recv.at[i], device(yy, cc, z, x))

    peers = [(dy, dc) for dy in (0, 1, 3, 2) for dc in (0, 1) if (dy, dc) != (0, 0)]
    own_lat = pltpu.make_async_copy(lat_hbm, lat.at[me], own_sem.at[0])
    own_q = pltpu.make_async_copy(
        q_hbm.at[:, pl.ds(pl.multiple_of(me * QW, 128), QW)], qbuf.at[me], own_sem.at[1]
    )
    own_lat.start()
    own_q.start()
    greet(exp_targets(y, core, z, x) + [device(step(y, d), 1 - core, z, x) for d in (1, 2, 3)])
    for dy in (1, 3, 2):
        lat_copy(dy).start()
    for dy, dc in peers:
        q_copy(dy, dc).start()
    stream_copy.start()

    def load_wo(j, carry):
        for side in range(2):
            wo_copy(j, side).start()
        return carry

    stream_send = remote(
        stream_hbm.at[:, half_of(1 - core)], sx.at[core], st_sem.at[0], st_sem.at[1], sibling
    )
    stream_send.start()
    stream_copy.wait()

    def rows_of(which):
        return pl.ds(pl.multiple_of(which * CHIP, CHIP), CHIP)

    def core_sum(j, send, recv):
        slot = lax.rem(j, 2)
        return remote(p_sib.at[slot], r_core.at[slot], send.at[j], recv.at[j], sibling)

    def scatter(j, send, recv):
        return [
            remote(
                p_own.at[lax.rem(j, SLOTS), rows_of(step(y, d))],
                rs_buf.at[lax.rem(j, SLOTS), d - 1],
                send.at[j, d],
                recv.at[j, d],
                device(step(y, d), core, z, x),
            )
            for d in (1, 3, 2)
        ]

    def spread(j):
        block = hbuf.at[j, core, y, :, 0:64]
        return [
            remote(block, block, ag_s.at[j, d], ag_r.at[j, d], device(step(y, d), core, z, x))
            for d in (1, 3, 2)
        ]

    def core_share(j):
        block = hbuf.at[j, core, :, :, 0:64]
        return remote(block, block, c2_s.at[j], c2_r.at[j], sibling)

    def gather_row():
        row = lax.broadcasted_iota(jnp.int32, (1152, 128), 0)
        low = lax.broadcasted_iota(jnp.int32, (1152, 128), 1) * ROWS
        inside = (row >= low) & (row < low + ROWS)
        member = jnp.where(inside, 1.0, 0.0).astype(BF)
        at = jnp.sum(jnp.where(inside, row - low, 0).astype(F32), axis=1, keepdims=True)
        return member, at

    def route_spots():
        lane = lax.broadcasted_iota(jnp.int32, (TOK, 128), 1)
        first = ((y * 2 + core) * 16).astype(F32)
        wanted = jnp.where(lane < 16, lane.astype(F32) + first, -1.0)
        earlier = lax.broadcasted_iota(jnp.int32, (TOK, 128), 0) > lane
        earlier = jnp.where(earlier, 1.0, 0.0).astype(BF)
        for b in range(8):
            rows = slice(b * TOK, (b + 1) * TOK)
            route = lat[b, :, KVL:].astype(F32)
            named = jnp.zeros((TOK, 128), F32)
            gate = jnp.zeros((TOK, 128), F32)
            for k in range(TOPK):
                hit = route[:, 64 + k : 65 + k] == wanted
                named = jnp.where(hit, 1.0, named)
                gate = jnp.where(hit, route[:, 64 + TOPK + k : 65 + TOPK + k], gate)
            slot = jnp.dot(earlier, named.astype(BF), preferred_element_type=F32)
            spots[0, rows, :] = jnp.where(named > 0.0, slot + (b * CAP), -1.0).astype(BF)
            spots[1, rows, :] = gate.astype(BF)

    def pickers_in():
        member, at = gather_row()
        for b in range(RING):
            rows = slice(b * 288, (b + 1) * 288)
            wide = lax.dot_general(
                member[rows], spots[0], (((1,), (1,)), ((), ())), preferred_element_type=F32
            )
            pickers[rows, 0:LEN] = jnp.where(wide == at[rows], 1.0, 0.0).astype(BF)

    def pickers_out():
        low = lax.broadcasted_iota(jnp.int32, (128, 1152), 0) * ROWS
        row = lax.broadcasted_iota(jnp.int32, (128, 1152), 1)
        inside = (row >= low) & (row < low + ROWS)
        member = jnp.where(inside, 1.0, 0.0).astype(BF)
        at = jnp.sum(jnp.where(inside, row - low, 0).astype(F32), axis=0, keepdims=True)
        for b in range(RING):
            rows = slice(b * CHIP, (b + 1) * CHIP)
            wide = jnp.dot(spots[0, rows, :], member, preferred_element_type=F32)
            gate = jnp.dot(spots[1, rows, :], member, preferred_element_type=F32)
            pickers[rows, :] = jnp.where(wide == at, gate, 0.0).astype(BF)

    def attention(kbuf, vbuf, uk_ref, uv_ref, u_sem):
        projections = [
            pltpu.make_async_copy(uk_hbm, uk_ref, u_sem.at[0]),
            pltpu.make_async_copy(uv_hbm, uv_ref, u_sem.at[1]),
        ]
        start_all(projections)
        own_lat.wait()
        lat_share(0).start()
        for dy in (1, 3, 2):
            lat_copy(4 - dy).wait_recv()
            lat_share(dy).start()
        for dy in (0, 1, 3, 2):
            lat_share(dy).wait()
        for dy in (1, 3, 2):
            lat_copy(dy).wait_send()
        own_q.wait()
        lax.fori_loop(0, CHUNKS, load_wo, 0)
        start_all(weights)

        wait_all(projections)
        lane = lax.broadcasted_iota(jnp.int32, (CHIP, 128), 1)

        def project(b, carry):
            rows = pl.ds(pl.multiple_of(b * CHIP, CHIP), CHIP)
            block = lat[pl.ds(b * 2, 2)].reshape(CHIP, LATW)
            latent = block[:, :KVL]
            rope = block[:, KVL:].astype(F32)
            rope_low = jnp.where(lane < 64, rope, 0.0).astype(BF)
            rope_high = pltpu.roll(rope, 64, 1)
            for h in range(8):
                nope = jnp.dot(latent, uk_ref[:, h * 128 : h * 128 + 128], preferred_element_type=F32)
                if h % 2 == 0:
                    kbuf[h, rows, 0:128] = nope.astype(BF)
                    kbuf[h, rows, 128:256] = rope_low
                else:
                    turned = pltpu.roll(nope, 64, 1)
                    kbuf[h, rows, 0:128] = jnp.where(lane < 64, 0.0, turned).astype(BF)
                    kbuf[h, rows, 128:256] = jnp.where(lane < 64, turned, rope_high).astype(BF)
            vbuf[rows, :] = jnp.dot(latent, uv_ref[...], preferred_element_type=F32).astype(BF)
            return carry

        lax.fori_loop(0, RING, project, 0)

        route_spots()
        pickers_in()
        factor = 1.0 / math.sqrt(NOPE + ROPE) * math.log2(math.e)
        row_at = lax.broadcasted_iota(jnp.int32, (CHIP, CHIP), 0)
        col_at = lax.broadcasted_iota(jnp.int32, (CHIP, CHIP), 1)
        causal = row_at >= col_at

        def attend(block):
            length = (block + 1) * CHIP

            def pair(p, carry):
                columns = pl.ds(pl.multiple_of(p * 384, 128), 384)
                q = qbuf[block * 2 : block * 2 + 2, :, columns].reshape(CHIP, 384)
                outs = []
                for odd in range(2):
                    query = q[:, odd * 128 : odd * 128 + 256]
                    head = p * 2 + odd
                    contract = (((1,), (1,)), ((), ()))
                    last = lax.dot_general(
                        query, kbuf[head, length - CHIP : length], contract, preferred_element_type=F32
                    )
                    last = jnp.where(causal, last, -jnp.inf)
                    peak = jnp.max(last, axis=1, keepdims=True)
                    if block:
                        first = lax.dot_general(
                            query, kbuf[head, 0 : length - CHIP], contract, preferred_element_type=F32
                        )
                        peak = jnp.maximum(peak, jnp.max(first, axis=1, keepdims=True))
                    values = pl.ds(pl.multiple_of(head * 128, 128), 128)
                    weight = jnp.exp2((last - peak) * factor)
                    total = jnp.sum(weight, axis=1, keepdims=True)
                    result = jnp.dot(
                        weight.astype(BF), vbuf[length - CHIP : length, values], preferred_element_type=F32
                    )
                    if block:
                        weight = jnp.exp2((first - peak) * factor)
                        total += jnp.sum(weight, axis=1, keepdims=True)
                        result += jnp.dot(
                            weight.astype(BF), vbuf[0 : length - CHIP, values], preferred_element_type=F32
                        )
                    outs.append((result / total).astype(BF))
                mixed[block * CHIP : (block + 1) * CHIP, pl.ds(pl.multiple_of(p * 256, 256), 256)] = (
                    jnp.concatenate(outs, axis=1)
                )
                return carry

            lax.fori_loop(0, 4, pair, 0)

        for dy in (0, 1, 3, 2):
            for dc in range(2):
                if (dy, dc) != (0, 0):
                    q_copy((4 - dy) % 4, dc).wait_recv()
            source = lax.rem(y + dy, RING)
            for block in range(RING):
                pl.when(source == block)(functools.partial(attend, block))
        for dy, dc in peers:
            q_copy(dy, dc).wait_send()

    pl.run_scoped(
        attention,
        pltpu.VMEM((8, LEN, 256), BF),
        pltpu.VMEM((LEN, 1024), BF),
        pltpu.VMEM((KVL, 1024), BF),
        pltpu.VMEM((KVL, 1024), BF),
        DMA((2,)),
    )
    stream_send.wait()

    def experts(units, squares):
        def one(j):
            return first_phase(j, spot, gs, t1, p1_s, p1_r, o1)

        def two(j):
            return second_phase(j, spot, t1, xbuf, lax.rem(j, ROWS_IN), p2_s, p2_r, o2)

        def project(j):
            for side in range(2):
                wo_copy(j, side).wait()
            own = late[j, 0, :, :, 0:64].reshape(1024, CW)
            other = late[j, 1, :, :, 0:64].reshape(1024, CW)
            both = jnp.concatenate([own, other], axis=1)

            def block(b, carry):
                rows = rows_of(b)
                product = jnp.dot(mixed[rows, :], both, preferred_element_type=F32).astype(BF)
                p_own[lax.rem(j, SLOTS), rows] = product[:, :CW]
                p_sib[lax.rem(j, 2), rows] = product[:, CW:]
                return carry

            lax.fori_loop(0, RING, block, 0)
            core_sum(j, c1_s, c1_r).start()

        def add_core(j):
            core_sum(j, c1_s, c1_r).wait()
            slot = lax.rem(j, SLOTS)
            p_own[slot] = (p_own[slot].astype(F32) + r_core[lax.rem(j, 2)].astype(F32)).astype(BF)
            start_all(scatter(j, rs_s, rs_r))

        def chip_total(j):
            slot = lax.rem(j, SLOTS)
            total = p_own[slot, rows_of(y)].astype(F32)
            for i in range(3):
                total += rs_buf[slot, i].astype(F32)
            return total

        def finish_hidden(j):
            wait_all(scatter(j, rs_s, rs_r))
            stream = sx[:, :, pl.ds(pl.multiple_of(j * CW, 128), CW)].reshape(CHIP, CW)
            hidden = (stream.astype(F32) + chip_total(j)).astype(BF)
            hbuf[j, core, y, :, 0:64] = hidden.reshape(RING, 64, CW)
            hown[j] = hidden
            start_all(spread(j))

        def share(j):
            wait_all(spread(j))
            core_share(j).start()

        def pick(j):
            core_share(j).wait()
            both = jnp.concatenate(
                [hbuf[j, half, :, :, 0:64].reshape(1024, CW) for half in range(2)], axis=1
            )

            def block(b, carry):
                left = pickers[pl.ds(pl.multiple_of(b * 288, 16), 288), 0:LEN]
                picked = jnp.dot(left, both, preferred_element_type=F32).reshape(RING, ROWS, 2 * CW)
                gs[lax.rem(j, SLOTS), 0, b] = picked[:, :, :CW].astype(BF)
                gs[lax.rem(j, SLOTS), 1, b] = picked[:, :, CW:].astype(BF)
                return carry

            lax.fori_loop(0, RING, block, 0)
            start_all(one(j))

        def forward(j):
            wait_all(one(j))
            start_all(two(j))

        def drain(j):
            wait_all(two(j))

            @pl.when(j == 0)
            def _():
                wait_all(weights)

            gains = [gain_ref[pl.ds(half * CHUNKS + j, 1), :] for half in range(2)]
            firsts = [pl.ds(pl.multiple_of(half * HALF + j * CW, 128), CW) for half in range(2)]
            right_gate = jnp.concatenate([wg[rows, :] for rows in firsts], axis=0)
            right_up = jnp.concatenate([wu[rows, :] for rows in firsts], axis=0)

            def block(b, carry):
                rows = pl.ds(pl.multiple_of(b * 288, 16), 288)
                parts = [xbuf[lax.rem(j, ROWS_IN), half, b].astype(F32).reshape(288, CW) for half in range(2)]
                squares[rows, :] += parts[0] * parts[0] + parts[1] * parts[1]
                left = jnp.concatenate([(p * g).astype(BF) for p, g in zip(parts, gains)], axis=1)
                units[rows, 0:FF] += jnp.dot(left, right_gate, preferred_element_type=F32)
                units[rows, FF : 2 * FF] += jnp.dot(left, right_up, preferred_element_type=F32)
                return carry

            lax.fori_loop(0, RING, block, 0)

        def clear():
            units[...] = jnp.zeros((1152, 2 * FF), F32)
            squares[...] = jnp.zeros((1152, CW), F32)

        def prepare(j):
            pl.when(j == 2)(clear)

        pipeline(
            [
                (0, project),
                (1, add_core),
                (1, prepare),
                (3, finish_hidden),
                (5, share),
                (6, pick),
                (8, forward),
                (10, drain),
            ]
        )

        def hidden_units(b, carry):
            rows = pl.ds(pl.multiple_of(b * 144, 16), 144)
            total = jnp.sum(squares[rows, :], axis=1, keepdims=True)
            scale = lax.rsqrt(total * (1.0 / D) + 1e-06)
            gate = units[rows, 0:FF] * scale
            up = units[rows, FF : 2 * FF] * scale
            mixed[rows, 0:FF] = (gate / (1.0 + jnp.exp(-gate)) * up).astype(BF)
            return carry

        lax.fori_loop(0, 8, hidden_units, 0)

        def back_one(j):
            return first_phase(j, spot, gs, late, d1_s, d1_r, o3)

        def back_two(j):
            return second_phase(j, spot, late, hbuf, j, d2_s, d2_r, o4)

        def exchange(j):
            slot = lax.rem(j, 2)
            return remote(swap.at[slot, 0], swap.at[slot, 1], sw_s.at[j], sw_r.at[j], sibling)

        def down(j):
            both = jnp.concatenate([wd[:, columns(half, j)] for half in range(2)], axis=1)

            def block(b, carry):
                left = mixed[pl.ds(pl.multiple_of(b * 288, 16), 288), 0:FF]
                result = jnp.dot(left, both, preferred_element_type=F32).reshape(RING, ROWS, 2 * CW)
                gs[lax.rem(j, SLOTS), 0, b] = result[:, :, :CW].astype(BF)
                gs[lax.rem(j, SLOTS), 1, b] = result[:, :, CW:].astype(BF)
                return carry

            lax.fori_loop(0, RING, block, 0)
            start_all(back_one(j))

        def back_forward(j):
            wait_all(back_one(j))
            start_all(back_two(j))

        def combine(j):
            wait_all(back_two(j))
            both = jnp.concatenate(
                [
                    hbuf[j, core].astype(F32).reshape(1152, CW).astype(BF),
                    hbuf[j, 1 - core].astype(F32).reshape(1152, CW).astype(BF),
                ],
                axis=1,
            )

            def block(b, carry):
                rows = rows_of(b)
                product = jnp.dot(pickers[rows, :], both, preferred_element_type=F32).astype(BF)
                p_own[lax.rem(j, SLOTS), rows] = product[:, :CW]
                p_sib[lax.rem(j, 2), rows] = product[:, CW:]
                return carry

            lax.fori_loop(0, RING, block, 0)
            core_sum(j, c3_s, c3_r).start()

        def add_back(j):
            core_sum(j, c3_s, c3_r).wait()
            slot = lax.rem(j, SLOTS)
            p_own[slot] = (p_own[slot].astype(F32) + r_core[lax.rem(j, 2)].astype(F32)).astype(BF)
            start_all(scatter(j, fs_s, fs_r))

        def finish(j):
            wait_all(scatter(j, fs_s, fs_r))
            total = (hown[j].astype(F32) + chip_total(j)).astype(BF)
            swap[lax.rem(j, 2), 0] = jnp.where(core == 0, total[TOK:], total[:TOK])
            exchange(j).start()
            out_ref[:, columns(core, j)] = jnp.where(core == 0, total[:TOK], total[TOK:])

        def land(j):
            exchange(j).wait()
            out_ref[:, columns(1 - core, j)] = swap[lax.rem(j, 2), 1]

        def prepare_back(j):
            pl.when(j == 0)(pickers_out)

        pipeline(
            [
                (0, down),
                (1, prepare_back),
                (2, back_forward),
                (4, combine),
                (5, add_back),
                (7, finish),
                (8, land),
            ]
        )

    pl.run_scoped(experts, pltpu.VMEM((1152, 2 * FF), F32), pltpu.VMEM((1152, CW), F32))


def moe_call(queries, packed, w_uk, w_uv, w_o, stream, w_gate, w_up, w_down, gain):
    grid_rows = (CHUNKS, 2, RING, RING, ROWS, CW)
    one = DMA((CHUNKS,))
    ring = DMA((CHUNKS, 4))
    phase = DMA((CHUNKS, 7))
    return pl.pallas_call(
        moe_kernel,
        out_shape=jax.ShapeDtypeStruct((TOK, D), BF),
        in_specs=[ANY] * 9 + [VM],
        out_specs=VM,
        scratch_shapes=[
            pltpu.VMEM((8, TOK, QW), BF),
            pltpu.VMEM((8, TOK, LATW), BF),
            *[DMA((8,))] * 4,
            DMA((2,)),
            pltpu.VMEM((1152, 1024), BF),
            pltpu.VMEM(grid_rows, BF),
            pltpu.VMEM((SLOTS, LEN, CW), BF),
            pltpu.VMEM((2, LEN, CW), BF),
            pltpu.VMEM((2, LEN, CW), BF),
            pltpu.VMEM((SLOTS, 3, CHIP, CW), BF),
            pltpu.VMEM(grid_rows, BF),
            pltpu.VMEM((SLOTS, *grid_rows[1:]), BF),
            pltpu.VMEM(grid_rows, BF),
            pltpu.VMEM((ROWS_IN, *grid_rows[1:]), BF),
            pltpu.VMEM((1152, 1152), BF),
            pltpu.VMEM((D, FF), BF),
            pltpu.VMEM((D, FF), BF),
            pltpu.VMEM((FF, D), BF),
            pltpu.VMEM((2, TOK, HALF), BF),
            pltpu.VMEM((CHUNKS, CHIP, CW), BF),
            pltpu.VMEM((2, 2, TOK, CW), BF),
            pltpu.VMEM((2, LEN, 128), BF),
            DMA((2,)),
            DMA((CHUNKS, 2)),
            DMA((3,)),
            DMA((2,)),
            *[one, one, ring, ring, ring, ring, one, one],
            *[phase] * 8,
            *[one, one, ring, ring, one, one],
            *[DMA((CHUNKS, 2))] * 4,
        ],
        compiler_params=pltpu.CompilerParams(
            collective_id=2, has_side_effects=True, vmem_limit_bytes=63 * 2**20
        ),
        name="moe",
    )(queries, packed, w_uk, w_uv, w_o, stream, w_gate, w_up, w_down, gain)


def local(
    stream_in,
    queries,
    latents,
    key_rope,
    w_uk,
    w_uv,
    w_o,
    norm_gain,
    expert_ids,
    gate_weights,
    w_gate,
    w_up,
    w_down,
):
    packed = jnp.concatenate(
        [latents[0], key_rope[0], expert_ids[0].astype(BF), gate_weights[0].astype(BF), jnp.zeros((TOK, 52), BF)],
        axis=1,
    )
    blocks = w_o.reshape(RING, RING, 64, D)
    out = moe_call(
        queries[0],
        packed,
        w_uk,
        w_uv,
        blocks,
        stream_in[0],
        w_gate[0],
        w_up[0],
        w_down[0],
        norm_gain.reshape(2 * CHUNKS, CW),
    )
    return out[None]


def solution(mesh):
    return jax.shard_map(
        local,
        mesh=mesh,
        in_specs=(
            P("exp", "ctx", None),
            P("exp", "ctx", None),
            P("exp", "ctx", None),
            P("exp", "ctx", None),
            P(None, "ctx"),
            P(None, "ctx"),
            P("ctx", None),
            P(),
            P("exp", "ctx", None),
            P("exp", "ctx", None),
            P(("ctx", "exp"), None, None),
            P(("ctx", "exp"), None, None),
            P(("ctx", "exp"), None, None),
        ),
        out_specs=P("exp", "ctx", None),
        check_vma=False,
    )
```

time: 249 us -> 242 us (0.972)
  Pallas kernels: 237 us -> 233 us
  local copies, waits for them, and re-layouts: 9.89 us -> 6.08 us
    pallas_call x1 -> x0, Pallas kernels: 50.4 us -> none  [attention_call(): pl.pallas_call(attention_kernel, out_shape=(jax.ShapeDtypeStruct((LEN, 10...]
    pallas_call x1, Pallas kernels: 186 us -> 233 us  [moe_call(): pl.pallas_call(moe_kernel, out_shape=jax.ShapeDtypeStruct((TOK, D), BF),...]
    unnamed x12 -> x4, local copies, waits for them, and re-layouts: 8.86 us -> 4.4 us
where the time goes in v4:
time: 242 us; the launch traced here: 239 us
  Pallas kernels  233 us (96%)
  local copies, waits for them, and re-layouts  6.08 us (3%)
    pallas_call x1, Pallas kernels, moe_call(): pl.pallas_call(moe_kernel, out_shape=jax.ShapeDtypeStruct((TOK, D), BF),...  233 us

profile of v4, /device:TPU:34, one launch (start us, length us, event | category | flops | bytes accessed | tf_op | source)
XLA Modules:
  0.0 238.8 jit_solution(10975982936790581946)
XLA Ops:
  0.0 0.8 copy.14
  0.8 0.8 copy.16
  1.6 0.8 copy.15
  2.5 1.7 concatenate.3.lat_hbm
  4.1 232.7 %moe.1 = bf16[128,2560]{1,0:T(8,128)(2,1)} custom-call(bf16[128,12288]{1,0:T(8,128)(2,1)} %bitcast.19, bf16[128,640]{1,0:T(8,128)(2,1)} %concatenate.3.lat_hbm, bf16[512,1024]{1,0:T(8,128)(2,1)} %uk_hbm.1, bf16[512,1024]{1,0:T(8,128)(2,1)} %uv_hbm.1, bf16[4,4,64,2560]{3,2,1,0:T(8,128)(2,1)} %bitcast.15, bf16[128,2560]{1,0:T(8,128)(2,1)} %bitcast.21, ...), custom_call_target="tpu_custom_call" | custom-call | tf_op jit(solution)/shard_map/moe/pallas_call | solution.py:608
  236.8 2.0 copy.18
  (2 shorter events, 0.0 us)

commit v5 on v4

--- a/solution.py
+++ b/solution.py
@@ -56,10 +56,11 @@
     )
 
 
-def greet(targets):
+def greet(targets, meanwhile):
     barrier = pltpu.get_barrier_semaphore()
     for target in targets:
         pl.semaphore_signal(barrier, inc=1, device_id=target, device_id_type=MESH)
+    meanwhile()
     pl.semaphore_wait(barrier, len(targets))
 
 
@@ -138,8 +139,9 @@
 
 
 def moe_kernel(
-    q_hbm, lat_hbm, uk_hbm, uv_hbm, wo_hbm, stream_hbm, wg_hbm, wu_hbm, wd_hbm, gain_ref, out_ref,
-    qbuf, lat, q_send, q_recv, l_send, l_recv, own_sem,
+    q_hbm, lat_hbm, uk_hbm, uv_hbm, wo_hbm, stream_hbm, wg_hbm, wu_hbm, wd_hbm,
+    gain_ref, rope_ref, ids_ref, gates_ref, out_ref,
+    qbuf, lat, turned, q_send, q_recv, l_send, l_recv, own_sem,
     mixed, late, p_own, p_sib, r_core, rs_buf, hbuf, gs, t1, xbuf, pickers, wg, wu, wd, sx, hown, swap, spots,
     in_sem, wo_sem, w_sem, st_sem, c1_s, c1_r, rs_s, rs_r, ag_s, ag_r, c2_s, c2_r, p1_s, p1_r, p2_s, p2_r,
     d1_s, d1_r, d2_s, d2_r, c3_s, c3_r, fs_s, fs_r, sw_s, sw_r, o1, o2, o3, o4,
@@ -169,7 +171,7 @@
     me = y * 2 + core
 
     def lat_copy(dy):
-        return remote(lat_hbm, lat.at[me], l_send.at[dy], l_recv.at[dy], device(step(y, dy), core, z, x))
+        return remote(lat.at[me], lat.at[me], l_send.at[dy], l_recv.at[dy], device(step(y, dy), core, z, x))
 
     def lat_share(dy):
         block = lat.at[step(y, dy) * 2 + core]
@@ -182,13 +184,25 @@
         return remote(q_hbm.at[:, columns], qbuf.at[me], q_send.at[i], q_recv.at[i], device(yy, cc, z, x))
 
     peers = [(dy, dc) for dy in (0, 1, 3, 2) for dc in (0, 1) if (dy, dc) != (0, 0)]
-    own_lat = pltpu.make_async_copy(lat_hbm, lat.at[me], own_sem.at[0])
+    own_lat = pltpu.make_async_copy(lat_hbm, lat.at[me, :, 0:KVL], own_sem.at[0])
     own_q = pltpu.make_async_copy(
         q_hbm.at[:, pl.ds(pl.multiple_of(me * QW, 128), QW)], qbuf.at[me], own_sem.at[1]
     )
     own_lat.start()
     own_q.start()
-    greet(exp_targets(y, core, z, x) + [device(step(y, d), 1 - core, z, x) for d in (1, 2, 3)])
+
+    def pack_side():
+        turned[...] = jnp.zeros((128, TOK), F32)
+        turned[0:ROPE, :] = rope_ref[...].astype(F32)
+        for k in range(TOPK):
+            turned[ROPE + k : ROPE + k + 1, :] = ids_ref[k].astype(F32)
+            turned[ROPE + TOPK + k : ROPE + TOPK + k + 1, :] = gates_ref[k]
+        lat[me, :, KVL:LATW] = jnp.transpose(turned[...]).astype(BF)
+        own_lat.wait()
+
+    greet(
+        exp_targets(y, core, z, x) + [device(step(y, d), 1 - core, z, x) for d in (1, 2, 3)], pack_side
+    )
     for dy in (1, 3, 2):
         lat_copy(dy).start()
     for dy, dc in peers:
@@ -290,7 +304,6 @@
             pltpu.make_async_copy(uv_hbm, uv_ref, u_sem.at[1]),
         ]
         start_all(projections)
-        own_lat.wait()
         lat_share(0).start()
         for dy in (1, 3, 2):
             lat_copy(4 - dy).wait_recv()
@@ -600,7 +613,7 @@
     pl.run_scoped(experts, pltpu.VMEM((1152, 2 * FF), F32), pltpu.VMEM((1152, CW), F32))
 
 
-def moe_call(queries, packed, w_uk, w_uv, w_o, stream, w_gate, w_up, w_down, gain):
+def moe_call(queries, latents, w_uk, w_uv, w_o, stream, w_gate, w_up, w_down, gain, rope, ids, gates):
     grid_rows = (CHUNKS, 2, RING, RING, ROWS, CW)
     one = DMA((CHUNKS,))
     ring = DMA((CHUNKS, 4))
@@ -608,11 +621,12 @@
     return pl.pallas_call(
         moe_kernel,
         out_shape=jax.ShapeDtypeStruct((TOK, D), BF),
-        in_specs=[ANY] * 9 + [VM],
+        in_specs=[ANY] * 9 + [VM] * 4,
         out_specs=VM,
         scratch_shapes=[
             pltpu.VMEM((8, TOK, QW), BF),
             pltpu.VMEM((8, TOK, LATW), BF),
+            pltpu.VMEM((128, TOK), F32),
             *[DMA((8,))] * 4,
             DMA((2,)),
             pltpu.VMEM((1152, 1024), BF),
@@ -646,7 +660,7 @@
             collective_id=2, has_side_effects=True, vmem_limit_bytes=63 * 2**20
         ),
         name="moe",
-    )(queries, packed, w_uk, w_uv, w_o, stream, w_gate, w_up, w_down, gain)
+    )(queries, latents, w_uk, w_uv, w_o, stream, w_gate, w_up, w_down, gain, rope, ids, gates)
 
 
 def local(
@@ -664,14 +678,10 @@
     w_up,
     w_down,
 ):
-    packed = jnp.concatenate(
-        [latents[0], key_rope[0], expert_ids[0].astype(BF), gate_weights[0].astype(BF), jnp.zeros((TOK, 52), BF)],
-        axis=1,
-    )
     blocks = w_o.reshape(RING, RING, 64, D)
     out = moe_call(
         queries[0],
-        packed,
+        latents[0],
         w_uk,
         w_uv,
         blocks,
@@ -680,6 +690,9 @@
         w_up[0],
         w_down[0],
         norm_gain.reshape(2 * CHUNKS, CW),
+        key_rope[0].T,
+        jnp.transpose(expert_ids, (2, 0, 1)),
+        jnp.transpose(gate_weights, (2, 0, 1)),
     )
     return out[None]
 

time: 242 us -> 238 us (0.983)
  local copies, waits for them, and re-layouts: 6.08 us -> 1.97 us
    unnamed x4 -> x1, local copies, waits for them, and re-layouts: 4.4 us -> 1.97 us
where the time goes in v5:
time: 238 us; the launch traced here: 234 us
  Pallas kernels  232 us (97%)
    pallas_call x1, Pallas kernels, moe_call(): pl.pallas_call(moe_kernel, out_shape=jax.ShapeDtypeStruct((TOK, D), BF),...  232 us

profile of v5, /device:TPU:34, one launch (start us, length us, event | category | flops | bytes accessed | tf_op | source)
XLA Modules:
  0.0 234.4 jit_solution(6778647890339157652)
XLA Ops:
  0.0 232.4 %moe.1 = bf16[128,2560]{1,0:T(8,128)(2,1)} custom-call(bf16[128,12288]{1,0:T(8,128)(2,1)} %bitcast.18, bf16[128,512]{1,0:T(8,128)(2,1)} %bitcast.21, bf16[512,1024]{1,0:T(8,128)(2,1)} %uk_hbm.1, bf16[512,1024]{1,0:T(8,128)(2,1)} %uv_hbm.1, bf16[4,4,64,2560]{3,2,1,0:T(8,128)(2,1)} %bitcast.14, bf16[128,2560]{1,0:T(8,128)(2,1)} %bitcast.20, ...), custom_call_target="tpu_custom_call" | custom-call | tf_op jit(solution)/shard_map/moe/pallas_call | solution.py:621
  232.4 2.0 copy.15

commit v6 on v5

--- a/solution.py
+++ b/solution.py
@@ -142,9 +142,9 @@
     q_hbm, lat_hbm, uk_hbm, uv_hbm, wo_hbm, stream_hbm, wg_hbm, wu_hbm, wd_hbm,
     gain_ref, rope_ref, ids_ref, gates_ref, out_ref,
     qbuf, lat, turned, q_send, q_recv, l_send, l_recv, own_sem,
-    mixed, late, p_own, p_sib, r_core, rs_buf, hbuf, gs, t1, xbuf, pickers, wg, wu, wd, sx, hown, swap, spots,
+    mixed, late, p_own, p_sib, r_core, rs_buf, hbuf, gs, t1, xbuf, pickers, wg, wu, wd, sx, hown, fs_buf, spots,
     in_sem, wo_sem, w_sem, st_sem, c1_s, c1_r, rs_s, rs_r, ag_s, ag_r, c2_s, c2_r, p1_s, p1_r, p2_s, p2_r,
-    d1_s, d1_r, d2_s, d2_r, c3_s, c3_r, fs_s, fs_r, sw_s, sw_r, o1, o2, o3, o4,
+    d1_s, d1_r, d2_s, d2_r, c3_s, c3_r, fs_s, fs_r, o1, o2, o3, o4,
 ):
     spot = place()
     y, core, z, x = spot
@@ -450,7 +450,6 @@
             stream = sx[:, :, pl.ds(pl.multiple_of(j * CW, 128), CW)].reshape(CHIP, CW)
             hidden = (stream.astype(F32) + chip_total(j)).astype(BF)
             hbuf[j, core, y, :, 0:64] = hidden.reshape(RING, 64, CW)
-            hown[j] = hidden
             start_all(spread(j))
 
         def share(j):
@@ -459,6 +458,8 @@
 
         def pick(j):
             core_share(j).wait()
+            for side, half in enumerate((core, 1 - core)):
+                hown[j, side] = hbuf[j, half, y, pl.ds(core * 2, 2), 0:64].reshape(TOK, CW)
             both = jnp.concatenate(
                 [hbuf[j, half, :, :, 0:64].reshape(1024, CW) for half in range(2)], axis=1
             )
@@ -537,9 +538,22 @@
         def back_two(j):
             return second_phase(j, spot, late, hbuf, j, d2_s, d2_r, o4)
 
-        def exchange(j):
-            slot = lax.rem(j, 2)
-            return remote(swap.at[slot, 0], swap.at[slot, 1], sw_s.at[j], sw_r.at[j], sibling)
+        def gather_back(j):
+            slot = lax.rem(j, SLOTS)
+            copies = []
+            for i, (dy, dc) in enumerate(peers):
+                yy, cc = step(y, dy), lax.rem(core + dc, 2)
+                rows = pl.ds(pl.multiple_of((yy * 2 + cc) * TOK, TOK), TOK)
+                copies.append(
+                    remote(
+                        p_own.at[slot, rows],
+                        fs_buf.at[slot, i],
+                        fs_s.at[j, i],
+                        fs_r.at[j, i],
+                        device(yy, cc, z, x),
+                    )
+                )
+            return copies
 
         def down(j):
             both = jnp.concatenate([wd[:, columns(half, j)] for half in range(2)], axis=1)
@@ -582,18 +596,18 @@
             core_sum(j, c3_s, c3_r).wait()
             slot = lax.rem(j, SLOTS)
             p_own[slot] = (p_own[slot].astype(F32) + r_core[lax.rem(j, 2)].astype(F32)).astype(BF)
-            start_all(scatter(j, fs_s, fs_r))
+            start_all(gather_back(j))
 
         def finish(j):
-            wait_all(scatter(j, fs_s, fs_r))
-            total = (hown[j].astype(F32) + chip_total(j)).astype(BF)
-            swap[lax.rem(j, 2), 0] = jnp.where(core == 0, total[TOK:], total[:TOK])
-            exchange(j).start()
-            out_ref[:, columns(core, j)] = jnp.where(core == 0, total[:TOK], total[TOK:])
-
-        def land(j):
-            exchange(j).wait()
-            out_ref[:, columns(1 - core, j)] = swap[lax.rem(j, 2), 1]
+            wait_all(gather_back(j))
+            slot = lax.rem(j, SLOTS)
+            mine = pl.ds(pl.multiple_of(me * TOK, TOK), TOK)
+            totals = [p_own[slot, mine].astype(F32), jnp.zeros((TOK, CW), F32)]
+            for i, (dy, dc) in enumerate(peers):
+                totals[dc] += fs_buf[slot, i].astype(F32)
+            for side, half in enumerate((core, 1 - core)):
+                hidden = hown[j, side].astype(F32)
+                out_ref[:, columns(half, j)] = (hidden + totals[side]).astype(BF)
 
         def prepare_back(j):
             pl.when(j == 0)(pickers_out)
@@ -606,7 +620,6 @@
                 (4, combine),
                 (5, add_back),
                 (7, finish),
-                (8, land),
             ]
         )
 
@@ -644,8 +657,8 @@
             pltpu.VMEM((D, FF), BF),
             pltpu.VMEM((FF, D), BF),
             pltpu.VMEM((2, TOK, HALF), BF),
-            pltpu.VMEM((CHUNKS, CHIP, CW), BF),
-            pltpu.VMEM((2, 2, TOK, CW), BF),
+            pltpu.VMEM((CHUNKS, 2, TOK, CW), BF),
+            pltpu.VMEM((SLOTS, 7, TOK, CW), BF),
             pltpu.VMEM((2, LEN, 128), BF),
             DMA((2,)),
             DMA((CHUNKS, 2)),
@@ -653,7 +666,8 @@
             DMA((2,)),
             *[one, one, ring, ring, ring, ring, one, one],
             *[phase] * 8,
-            *[one, one, ring, ring, one, one],
+            *[one, one],
+            *[DMA((CHUNKS, 7))] * 2,
             *[DMA((CHUNKS, 2))] * 4,
         ],
         compiler_params=pltpu.CompilerParams(

time: 238 us -> 237 us (level)
  no operation moved by 1% of the time
where the time goes in v6:
time: 237 us; the launch traced here: 234 us
  Pallas kernels  232 us (98%)
    pallas_call x1, Pallas kernels, moe_call(): pl.pallas_call(moe_kernel, out_shape=jax.ShapeDtypeStruct((TOK, D), BF),...  232 us

profile of v6, /device:TPU:34, one launch (start us, length us, event | category | flops | bytes accessed | tf_op | source)
XLA Modules:
  0.0 233.6 jit_solution(11271345612793588474)
XLA Ops:
  0.0 231.6 %moe.1 = bf16[128,2560]{1,0:T(8,128)(2,1)} custom-call(bf16[128,12288]{1,0:T(8,128)(2,1)} %bitcast.18, bf16[128,512]{1,0:T(8,128)(2,1)} %bitcast.21, bf16[512,1024]{1,0:T(8,128)(2,1)} %uk_hbm.1, bf16[512,1024]{1,0:T(8,128)(2,1)} %uv_hbm.1, bf16[4,4,64,2560]{3,2,1,0:T(8,128)(2,1)} %bitcast.14, bf16[128,2560]{1,0:T(8,128)(2,1)} %bitcast.20, ...), custom_call_target="tpu_custom_call" | custom-call | tf_op jit(solution)/shard_map/moe/pallas_call | solution.py:634
  231.7 2.0 copy.15

commit v7 on v6

--- a/solution.py
+++ b/solution.py
@@ -224,8 +224,9 @@
         return pl.ds(pl.multiple_of(which * CHIP, CHIP), CHIP)
 
     def core_sum(j, send, recv):
-        slot = lax.rem(j, 2)
-        return remote(p_sib.at[slot], r_core.at[slot], send.at[j], recv.at[j], sibling)
+        return remote(
+            p_sib.at[lax.rem(j, 2)], r_core.at[lax.rem(j, SLOTS)], send.at[j], recv.at[j], sibling
+        )
 
     def scatter(j, send, recv):
         return [
@@ -435,7 +436,7 @@
         def add_core(j):
             core_sum(j, c1_s, c1_r).wait()
             slot = lax.rem(j, SLOTS)
-            p_own[slot] = (p_own[slot].astype(F32) + r_core[lax.rem(j, 2)].astype(F32)).astype(BF)
+            p_own[slot] = (p_own[slot].astype(F32) + r_core[slot].astype(F32)).astype(BF)
             start_all(scatter(j, rs_s, rs_r))
 
         def chip_total(j):
@@ -506,7 +507,7 @@
             squares[...] = jnp.zeros((1152, CW), F32)
 
         def prepare(j):
-            pl.when(j == 2)(clear)
+            pl.when(j == 8)(clear)
 
         pipeline(
             [
@@ -595,7 +596,7 @@
         def add_back(j):
             core_sum(j, c3_s, c3_r).wait()
             slot = lax.rem(j, SLOTS)
-            p_own[slot] = (p_own[slot].astype(F32) + r_core[lax.rem(j, 2)].astype(F32)).astype(BF)
+            p_own[slot] = (p_own[slot].astype(F32) + r_core[slot].astype(F32)).astype(BF)
             start_all(gather_back(j))
 
         def finish(j):
@@ -616,10 +617,10 @@
             [
                 (0, down),
                 (1, prepare_back),
-                (2, back_forward),
-                (4, combine),
-                (5, add_back),
-                (7, finish),
+                (3, back_forward),
+                (5, combine),
+                (7, add_back),
+                (9, finish),
             ]
         )
 
@@ -646,7 +647,7 @@
             pltpu.VMEM(grid_rows, BF),
             pltpu.VMEM((SLOTS, LEN, CW), BF),
             pltpu.VMEM((2, LEN, CW), BF),
-            pltpu.VMEM((2, LEN, CW), BF),
+            pltpu.VMEM((SLOTS, LEN, CW), BF),
             pltpu.VMEM((SLOTS, 3, CHIP, CW), BF),
             pltpu.VMEM(grid_rows, BF),
             pltpu.VMEM((SLOTS, *grid_rows[1:]), BF),

time: 237 us -> 238 us (level)
  no operation moved by 1% of the time
where the time goes in v7:
time: 238 us; the launch traced here: 235 us
  Pallas kernels  233 us (98%)
    pallas_call x1, Pallas kernels, moe_call(): pl.pallas_call(moe_kernel, out_shape=jax.ShapeDtypeStruct((TOK, D), BF),...  233 us

profile of v7, /device:TPU:34, one launch (start us, length us, event | category | flops | bytes accessed | tf_op | source)
XLA Modules:
  0.0 235.0 jit_solution(10638604294740771121)
XLA Ops:
  0.0 233.0 %moe.1 = bf16[128,2560]{1,0:T(8,128)(2,1)} custom-call(bf16[128,12288]{1,0:T(8,128)(2,1)} %bitcast.18, bf16[128,512]{1,0:T(8,128)(2,1)} %bitcast.21, bf16[512,1024]{1,0:T(8,128)(2,1)} %uk_hbm.1, bf16[512,1024]{1,0:T(8,128)(2,1)} %uv_hbm.1, bf16[4,4,64,2560]{3,2,1,0:T(8,128)(2,1)} %bitcast.14, bf16[128,2560]{1,0:T(8,128)(2,1)} %bitcast.20, ...), custom_call_target="tpu_custom_call" | custom-call | tf_op jit(solution)/shard_map/moe/pallas_call | solution.py:635
  233.0 2.0 copy.15

commit v8 on v6

--- a/solution.py
+++ b/solution.py
@@ -340,8 +340,6 @@
 
         lax.fori_loop(0, RING, project, 0)
 
-        route_spots()
-        pickers_in()
         factor = 1.0 / math.sqrt(NOPE + ROPE) * math.log2(math.e)
         row_at = lax.broadcasted_iota(jnp.int32, (CHIP, CHIP), 0)
         col_at = lax.broadcasted_iota(jnp.int32, (CHIP, CHIP), 1)
@@ -506,7 +504,9 @@
             squares[...] = jnp.zeros((1152, CW), F32)
 
         def prepare(j):
-            pl.when(j == 2)(clear)
+            pl.when(j == 0)(route_spots)
+            pl.when(j == 4)(pickers_in)
+            pl.when(j == 8)(clear)
 
         pipeline(
             [

time: 237 us -> 238 us (level)
  no operation moved by 1% of the time
where the time goes in v8:
time: 238 us; the launch traced here: 235 us
  Pallas kernels  233 us (98%)
    pallas_call x1, Pallas kernels, moe_call(): pl.pallas_call(moe_kernel, out_shape=jax.ShapeDtypeStruct((TOK, D), BF),...  233 us

profile of v8, /device:TPU:34, one launch (start us, length us, event | category | flops | bytes accessed | tf_op | source)
XLA Modules:
  0.0 234.6 jit_solution(2816690868401332138)
XLA Ops:
  0.0 232.6 %moe.1 = bf16[128,2560]{1,0:T(8,128)(2,1)} custom-call(bf16[128,12288]{1,0:T(8,128)(2,1)} %bitcast.18, bf16[128,512]{1,0:T(8,128)(2,1)} %bitcast.21, bf16[512,1024]{1,0:T(8,128)(2,1)} %uk_hbm.1, bf16[512,1024]{1,0:T(8,128)(2,1)} %uv_hbm.1, bf16[4,4,64,2560]{3,2,1,0:T(8,128)(2,1)} %bitcast.14, bf16[128,2560]{1,0:T(8,128)(2,1)} %bitcast.20, ...), custom_call_target="tpu_custom_call" | custom-call | tf_op jit(solution)/shard_map/moe/pallas_call | solution.py:634
  232.6 2.0 copy.15
